TPU v7x, 32 devices: a whole 2x2x4 slice. The times are simulated.
32 devices in a mesh: seq: 4 (over x, core), blk: 8 (over z, y).
Axes of the slice: x: 2, y: 2, z: 4, core: 2. Of those that a mesh axis runs over, the one named last changes fastest.
Arguments:
- tokens: bfloat16 [4, 4096, 576], P('seq', 'blk'), may hold values from -6 to 6
- positions: int32 [4, 4096], P('seq', 'blk'), may hold values from 0 to 4095, as said below
- groups: int32 [4, 4096], P('seq', 'blk'), may hold values from 0 to 1
- keep_mask: int32 [4], P('seq'), may hold values from 0 to 1, as said below
- exit_scales: float32 [2], replicated, may hold values from 0.5 to 2
- keep_rate: float32 [1], replicated, may hold values from 1.1 to 2
- query_weight: bfloat16 [576, 576], replicated, may hold values from -0.25 to 0.25
- key_weight: bfloat16 [576, 192], replicated, may hold values from -0.25 to 0.25
- value_weight: bfloat16 [576, 192], replicated, may hold values from -0.25 to 0.25
- output_weight: bfloat16 [576, 576], replicated, may hold values from -4 to 4
- gate_weight: bfloat16 [576, 1536], replicated, may hold values from -0.25 to 0.25
- up_weight: bfloat16 [576, 1536], replicated, may hold values from -0.25 to 0.25
- down_weight: bfloat16 [1536, 576], replicated, may hold values from -0.15625 to 0.15625
- attention_gain: float32 [576], replicated, may hold values from 0.5 to 1.5
- feedforward_gain: float32 [576], replicated, may hold values from 0.5 to 1.5
- cotangent: bfloat16 [4, 4096, 576], P('seq', 'blk'), may hold values from -6 to 6
Outputs:
- layer_out: bfloat16 [4, 4096, 576], P('seq', 'blk')
- input_grad: float32 [4, 4096, 576], P('seq', 'blk')
- query_grad: float32 [576, 576], replicated
- key_grad: float32 [576, 192], replicated
- value_grad: float32 [576, 192], replicated
- output_grad: float32 [576, 576], replicated
- gate_grad: float32 [576, 1536], replicated
- up_grad: float32 [576, 1536], replicated
- down_grad: float32 [1536, 576], replicated
- attention_gain_grad: float32 [576], replicated
- feedforward_gain_grad: float32 [576], replicated
Inputs may be any that keep to these rules, and one draw needn't show every extreme that they name: Within a sequence positions count up by one and fall back to 0 where a packed document begins; in one sequence, drawn from the seed, they never fall back. `keep_mask`: at least one sequence, drawn from the seed, runs the layer, and at least one other skips it.
All inputs are finite; a program needn't handle non-finite values.
Results may differ from a plain program's by a relative error of at most 0.015.
Values may be sent and summed in bfloat16 or wider, within the bound.
A program may use at most 192 MiB of HBM per device.

v0:
```python
import math

import jax
import jax.numpy as jnp
from jax import lax
from jax.sharding import PartitionSpec as P

H = 9
KVH = 3
HD = 64


EPSILON = 1e-05
ROPE_BASE = 100000.0
MASKED = -1e30
BLOCK_KEYS = 1024


def angles(positions, head_size):
    halfway = head_size // 2
    frequency = 1.0 / ROPE_BASE ** (jnp.arange(halfway, dtype=jnp.float32) * (2.0 / head_size))
    turned = positions.astype(jnp.float32)[..., None] * frequency
    return (jnp.cos(turned), jnp.sin(turned))


def rotate(values, cosine, sine_vals):
    halfway = values.shape[-1] // 2
    front_half = values[..., :halfway]
    behind = values[..., halfway:]
    cos_part = cosine[:, :, None, :]
    sin_part = sine_vals[:, :, None, :]
    return jnp.concatenate(
        [front_half * cos_part - behind * sin_part, behind * cos_part + front_half * sin_part],
        axis=-1,
    )


def over_blocks(key_piece, first_key, carried, block_work, query_last):
    key_count = key_piece.shape[1]
    block_len = math.gcd(key_count, BLOCK_KEYS)

    def one_step(block_no, current):
        key_start = first_key + block_no * block_len
        key_block = lax.dynamic_slice_in_dim(key_piece, block_no * block_len, block_len, 1)
        return lax.cond(
            key_start <= query_last,
            lambda inner: block_work(inner, key_block, key_start),
            lambda inner: inner,
            current,
        )

    return lax.fori_loop(0, key_count // block_len, one_step, carried)


def block_scores(query_heads, key_block, key_start, query_pos, score_scale):
    seq_count, block_len, doubled = key_block.shape
    kv_width = doubled // 2
    kv_heads = query_heads.shape[2]
    head_size = query_heads.shape[4]
    key_heads = key_block[..., :kv_width].reshape(seq_count, block_len, kv_heads, head_size)
    value_heads = key_block[..., kv_width:].reshape(seq_count, block_len, kv_heads, head_size)
    scores = (
        jnp.einsum("sqkgd,stkd->skgqt", query_heads, key_heads, preferred_element_type=jnp.float32)
        * score_scale
    )
    causal = query_pos[:, None] >= (key_start + jnp.arange(block_len, dtype=jnp.int32))[None, :]
    return (scores, causal, key_heads, value_heads)


def body(
    tokens,
    positions,
    groups,
    keep_mask,
    exit_scales,
    keep_rate,
    query_weight,
    key_weight,
    value_weight,
    output_weight,
    gate_weight,
    up_weight,
    down_weight,
    attention_gain,
    feedforward_gain,
    cotangent,
):
    seq_count, row_count, model_width = tokens.shape
    group_size = H // KVH
    kv_width = KVH * HD
    score_scale = HD ** (-0.5)
    block_index = lax.axis_index("blk")
    query_pos = block_index * row_count + jnp.arange(row_count, dtype=jnp.int32)
    query_last = block_index * row_count + row_count - 1
    inputs = tokens.astype(jnp.float32)
    cosine, sine_vals = angles(positions, HD)
    branch_scale = (keep_mask.astype(jnp.float32) * keep_rate[0])[:, None, None]
    inv_first = lax.rsqrt(jnp.mean(inputs * inputs, axis=-1, keepdims=True) + EPSILON)
    normed = (inputs * inv_first * attention_gain).astype(jnp.bfloat16)
    query_raw = jnp.dot(normed, query_weight, preferred_element_type=jnp.float32)
    key_raw = jnp.dot(normed, key_weight, preferred_element_type=jnp.float32)
    value_raw = jnp.dot(normed, value_weight, preferred_element_type=jnp.float32)
    queries = rotate(query_raw.reshape(seq_count, row_count, H, HD), cosine, sine_vals).astype(
        jnp.bfloat16
    )
    query_heads = queries.reshape(seq_count, row_count, KVH, group_size, HD)
    keys_rot = rotate(key_raw.reshape(seq_count, row_count, KVH, HD), cosine, sine_vals).reshape(
        seq_count, row_count, kv_width
    )
    key_vals = jnp.concatenate([keys_rot, value_raw], axis=-1).astype(jnp.bfloat16)

    def stats_work(current, key_block, key_start):
        run_max, run_sum = current
        scores, causal, key_heads, value_heads = block_scores(
            query_heads, key_block, key_start, query_pos, score_scale
        )
        scores = jnp.where(causal, scores, MASKED)
        new_max = jnp.maximum(run_max, jnp.max(scores, axis=-1))
        fresh = jnp.sum(jnp.where(causal, jnp.exp(scores - new_max[..., None]), 0.0), axis=-1)
        return (new_max, run_sum * jnp.exp(run_max - new_max) + fresh)

    stat_shape = (seq_count, KVH, group_size, row_count)
    start_stats = (jnp.full(stat_shape, MASKED, jnp.float32), jnp.zeros(stat_shape, jnp.float32))
    run_max, run_sum = over_blocks(
        lax.all_gather(key_vals, "blk", axis=1, tiled=True),
        jnp.int32(0),
        start_stats,
        stats_work,
        query_last,
    )
    log_total = run_max + jnp.log(run_sum)

    def values_work(current, key_block, key_start):
        scores, causal, key_heads, value_heads = block_scores(
            query_heads, key_block, key_start, query_pos, score_scale
        )
        probability = jnp.where(causal, jnp.exp(scores - log_total[..., None]), 0.0).astype(
            jnp.bfloat16
        )
        return current + jnp.einsum(
            "skgqt,stkd->sqkgd", probability, value_heads, preferred_element_type=jnp.float32
        )

    start_acc = jnp.zeros((seq_count, row_count, KVH, group_size, HD), jnp.float32)
    attended = over_blocks(
        lax.all_gather(key_vals, "blk", axis=1, tiled=True),
        jnp.int32(0),
        start_acc,
        values_work,
        query_last,
    )
    mixed = attended.reshape(seq_count, row_count, H * HD).astype(jnp.bfloat16)
    branch = jnp.dot(mixed, output_weight, preferred_element_type=jnp.float32)
    hidden_state = inputs + branch_scale * branch
    inv_second = lax.rsqrt(jnp.mean(hidden_state * hidden_state, axis=-1, keepdims=True) + EPSILON)
    normed2 = (hidden_state * inv_second * feedforward_gain).astype(jnp.bfloat16)
    gate = jnp.dot(normed2, gate_weight, preferred_element_type=jnp.float32)
    up_proj = jnp.dot(normed2, up_weight, preferred_element_type=jnp.float32)
    sigmoid_gate = jax.nn.sigmoid(gate)
    silu_gate = gate * sigmoid_gate
    act = (silu_gate * up_proj).astype(jnp.bfloat16)
    down = jnp.dot(act, down_weight, preferred_element_type=jnp.float32)
    layer_out = (hidden_state + branch_scale * down).astype(jnp.bfloat16)
    group_scale = jnp.where(groups == 1, exit_scales[1], exit_scales[0])
    seed_grad = cotangent.astype(jnp.float32) * group_scale[..., None]
    d_down = (branch_scale * seed_grad).astype(jnp.bfloat16)
    down_grad = jnp.einsum("scf,scd->fd", act, d_down, preferred_element_type=jnp.float32)
    d_act = jnp.einsum("scd,fd->scf", d_down, down_weight, preferred_element_type=jnp.float32)
    d_gate = (d_act * up_proj * sigmoid_gate * (1.0 + gate * (1.0 - sigmoid_gate))).astype(
        jnp.bfloat16
    )
    d_up = (d_act * silu_gate).astype(jnp.bfloat16)
    gate_grad = jnp.einsum("scd,scf->df", normed2, d_gate, preferred_element_type=jnp.float32)
    up_grad = jnp.einsum("scd,scf->df", normed2, d_up, preferred_element_type=jnp.float32)
    d_normed2 = jnp.einsum(
        "scf,df->scd", d_gate, gate_weight, preferred_element_type=jnp.float32
    ) + jnp.einsum("scf,df->scd", d_up, up_weight, preferred_element_type=jnp.float32)
    feedforward_gain_grad = jnp.sum(d_normed2 * hidden_state * inv_second, axis=(0, 1))
    gained_two = feedforward_gain * d_normed2
    d_hidden = (
        seed_grad
        + inv_second * gained_two
        - hidden_state * inv_second**3 * jnp.mean(gained_two * hidden_state, axis=-1, keepdims=True)
    )
    d_branch = (branch_scale * d_hidden).astype(jnp.bfloat16)
    output_grad = jnp.einsum("scn,scd->nd", mixed, d_branch, preferred_element_type=jnp.float32)
    d_mixed = jnp.einsum(
        "scd,nd->scn", d_branch, output_weight, preferred_element_type=jnp.float32
    ).astype(jnp.bfloat16)
    d_heads = d_mixed.reshape(seq_count, row_count, KVH, group_size, HD)
    delta = jnp.einsum("sqkgd,sqkgd->skgq", d_heads.astype(jnp.float32), attended)

    def block_grads(key_block, key_start):
        scores, causal, key_heads, value_heads = block_scores(
            query_heads, key_block, key_start, query_pos, score_scale
        )
        probability = jnp.where(causal, jnp.exp(scores - log_total[..., None]), 0.0)
        d_prob = jnp.einsum(
            "sqkgd,stkd->skgqt", d_heads, value_heads, preferred_element_type=jnp.float32
        )
        d_scores = (probability * (d_prob - delta[..., None])).astype(jnp.bfloat16)
        query_part = (
            jnp.einsum("skgqt,stkd->sqkgd", d_scores, key_heads, preferred_element_type=jnp.float32)
            * score_scale
        )
        d_key_part = (
            jnp.einsum(
                "skgqt,sqkgd->stkd", d_scores, query_heads, preferred_element_type=jnp.float32
            )
            * score_scale
        )
        d_value_part = jnp.einsum(
            "skgqt,sqkgd->stkd",
            probability.astype(jnp.bfloat16),
            d_heads,
            preferred_element_type=jnp.float32,
        )
        block_len = key_block.shape[1]
        block_term = jnp.concatenate(
            [
                d_key_part.reshape(seq_count, block_len, kv_width),
                d_value_part.reshape(seq_count, block_len, kv_width),
            ],
            axis=-1,
        )
        return (query_part, block_term)

    def grads_work(current, key_block, key_start):
        d_query_acc, term = current
        query_part, block_term = block_grads(key_block, key_start)
        return (
            d_query_acc + query_part,
            lax.dynamic_update_slice_in_dim(term, block_term, key_start, 1),
        )

    gathered = lax.all_gather(key_vals, "blk", axis=1, tiled=True)
    start_query = jnp.zeros((seq_count, row_count, KVH, group_size, HD), jnp.float32)
    start_grads = (
        start_query,
        jnp.zeros((seq_count, gathered.shape[1], 2 * kv_width), jnp.float32),
    )
    d_query_acc, term = over_blocks(gathered, 0, start_grads, grads_work, query_last)
    kv_grad = lax.psum_scatter(
        term.astype(jnp.bfloat16), "blk", scatter_dimension=1, tiled=True
    ).astype(jnp.float32)
    d_query = (
        rotate(d_query_acc.reshape(seq_count, row_count, H, HD), cosine, -sine_vals)
        .reshape(seq_count, row_count, H * HD)
        .astype(jnp.bfloat16)
    )
    d_key = (
        rotate(kv_grad[..., :kv_width].reshape(seq_count, row_count, KVH, HD), cosine, -sine_vals)
        .reshape(seq_count, row_count, kv_width)
        .astype(jnp.bfloat16)
    )
    d_value = kv_grad[..., kv_width:].astype(jnp.bfloat16)
    query_grad = jnp.einsum("scd,scn->dn", normed, d_query, preferred_element_type=jnp.float32)
    key_grad = jnp.einsum("scd,scn->dn", normed, d_key, preferred_element_type=jnp.float32)
    value_grad = jnp.einsum("scd,scn->dn", normed, d_value, preferred_element_type=jnp.float32)
    d_normed = (
        jnp.einsum("scn,dn->scd", d_query, query_weight, preferred_element_type=jnp.float32)
        + jnp.einsum("scn,dn->scd", d_key, key_weight, preferred_element_type=jnp.float32)
        + jnp.einsum("scn,dn->scd", d_value, value_weight, preferred_element_type=jnp.float32)
    )
    attention_gain_grad = jnp.sum(d_normed * inputs * inv_first, axis=(0, 1))
    gained_one = attention_gain * d_normed
    input_grad = (
        d_hidden
        + inv_first * gained_one
        - inputs * inv_first**3 * jnp.mean(gained_one * inputs, axis=-1, keepdims=True)
    )
    summed = lax.psum(
        (
            query_grad,
            key_grad,
            value_grad,
            output_grad,
            gate_grad,
            up_grad,
            down_grad,
            attention_gain_grad,
            feedforward_gain_grad,
        ),
        ("seq", "blk"),
    )
    return (
        layer_out,
        input_grad,
        summed[0],
        summed[1],
        summed[2],
        summed[3],
        summed[4],
        summed[5],
        summed[6],
        summed[7],
        summed[8],
    )


def solution(mesh):
    placed = (
        P("seq", "blk", None),
        P("seq", "blk"),
        P("seq", "blk"),
        P("seq"),
        P(),
        P(),
        P(),
        P(),
        P(),
        P(),
        P(),
        P(),
        P(),
        P(),
        P(),
        P("seq", "blk", None),
    )
    return jax.shard_map(
        body,
        mesh=mesh,
        in_specs=placed,
        out_specs=(
            P("seq", "blk", None),
            P("seq", "blk", None),
            P(),
            P(),
            P(),
            P(),
            P(),
            P(),
            P(),
            P(),
            P(),
        ),
        check_vma=False,
    )
```

profile of v0, /device:TPU:0, one launch (start us, length us, event | category | flops | bytes accessed | tf_op | source)
XLA Modules:
  0.0 752.8 jit_solution(3254804453472322721)
XLA Ops:
  7.3 1.4 fusion.54
  9.2 1.6 fusion.67
  16.3 1.8 convolution_bitcast_fusion.1
  18.8 1.3 compare_select_fusion
  20.1 58.9 %all-gather.2.cloned.1.call-done = bf16[1,4096,384]{1,2,0:T(8,128)(2,1)} async-done(((bf16[1,512,384]{1,2,0:T(8,128)(2,1)}), bf16[1,4096,384]{1,2,0:T(8,128)(2,1)}) %all-gather.2.cloned.1.call-update) | async-done | bytes 3145744 | tf_op jit(solution)/shard_map/all_gather | solution.py:146
  79.1 20.6 %while.49 = (s32[]{:T(128)}, f32[1,3,3,512]{3,2,1,0:T(4,128)S(1)}, f32[1,3,3,512]{3,2,1,0:T(4,128)S(1)}, s32[]{:T(128)}, bf16[1,4096,384]{1,2,0:T(8,128)(2,1)}, ...) while((s32[]{:T(128)}, f32[1,3,3,512]{3,2,1,0:T(4,128)S(1)}, ...), condition=%wide.region_6.7_spmd.clone, body=%wide.region_1.6_spmd.clone.sunk | while | flops 642263552 | bytes 41347344 | solution.py:52
  79.1 20.4 %conditional.9 = ((f32[1,3,3,512]{3,2,1,0:T(4,128)S(1)}, f32[1,3,3,512]{3,2,1,0:T(4,128)S(1)})) conditional(s32[]{:T(128)} %convert_element_type.294, (f32[1,3,3,512]{3,2,1,0:T(4,128)S(1)}, f32[1,3,3,512]{3,2,1,0:T(4,128)S(1)}) %tuple.156, (s32[]{:T(128)}, s32[]{:T(128)}, bf16[1,4096,384]{1,2,0:T(8,128)(2,1)}, ...), branch_computations={%region_2.0_spmd, %region_3.5_spmd} | conditional | flops 642263552 | bytes 41345096 | solution.py:45
  80.5 8.1 %fusion.6 = (f32[3,3,512]{2,1,0:T(4,128)S(1)}, f32[3,1024,512,3]{2,1,3,0:T(8,128)}) fusion(pred[512,1024]{0,1:T(8,128)(4,1)S(1)} %broadcast_compare_fusion, bf16[1024,3,64,1]{0,2,3,1:T(8,128)(2,1)S(1)} %bitcast.291, bf16[1,512,3,3,64]{1,4,3,2,0:T(8,128)(2,1)S(1)} %get-tuple-element.607), kind=kOutput, calls=%fused_computation.5 | convolution fusion | flops 618130944 | bytes 20400128 | tf_op jit(solution)/shard_map/while/body/eval_jaxpr/cond/branch_1_fun/sqkgd,stkd->skgqt/dot_general | solution.py:63
  88.6 10.8 %select_reduce_fusion = f32[3,3,512]{2,1,0:T(4,128)S(1)} fusion(f32[3,1024,512,3]{2,1,3,0:T(8,128)} %get-tuple-element.808, f32[3,3,512]{2,1,0:T(4,128)S(1)} %bitcast.296, pred[512,1024]{0,1:T(8,128)(4,1)S(1)} %broadcast_compare_fusion), kind=kLoop, calls=%fused_computation.4 | loop fusion | flops 23588352 | bytes 19435520 | tf_op jit(solution)/shard_map/while/body/eval_jaxpr/cond/branch_1_fun/reduce_sum | solution.py:119
  100.8 10.2 %while.50 = (s32[]{:T(128)}, f32[1,512,3,3,64]{1,4,3,2,0:T(8,128)}, s32[]{:T(128)}, bf16[1,4096,384]{1,2,0:T(8,128)(2,1)}, bf16[1,512,3,3,64]{1,4,3,2,0:T(8,128)...) while((s32[]{:T(128)}, f32[1,512,3,3,64]{1,4,3,2,0:T(8,128)}, ...), condition=%wide.region_10.11_spmd.clone, body=%wide.region_7.10_spmd.clone.sunk | while | flops 1227654656 | bytes 6392061 | solution.py:52
  101.0 10.0 %conditional.10 = (f32[1,512,3,3,64]{1,4,3,2,0:T(8,128)}) conditional(s32[]{:T(128)} %convert_element_type.295, f32[1,512,3,3,64]{1,4,3,2,0:T(8,128)} %get-tuple-element.1037, (s32[]{:T(128)}, bf16[1,4096,384]{1,2,0:T(8,128)(2,1)}, s32[]{:T(128)}, bf16[1,512,3,3,64]{1,4,3,2,0:T(8,128)(2,1)S(1)}, f32[1,3,3,512]{3,2,1,0:T(4,128)S(1)}, ...), branch_computations={%region_8.8_spmd, %region_9.9_spmd} | conditional | flops 1227654656 | bytes 6389830 | solution.py:45
  101.0 1.9 constant_dynamic-slice_fusion.2
  103.3 7.7 %fusion.21 = f32[1,512,3,3,64]{1,4,3,2,0:T(8,128)} fusion(f32[1,512,3,3,64]{1,4,3,2,0:T(8,128)} %get-tuple-element.619, bf16[1024,3,64,1]{0,2,3,1:T(8,128)(2,1)} %bitcast.293, f32[3,3,512]{2,1,0:T(4,128)S(1)} %bitcast.316, pred[512,1024]{0,1:T(8,128)(4,1)S(1)} %broadcast_compare_fusion.1, bf16[1024,3,64,1]{0,2,3,1:T(8,128)(2,1)S(1)} %bitcast.292, ...), kind=kOutput, calls=%fused_computation.23 | convolution fusion | flops 1227128832 | bytes 4278272 | tf_op jit(solution)/shard_map/while/body/eval_jaxpr/cond/branch_1_fun/skgqt,stkd->sqkgd/dot_general | solution.py:140
  111.1 1.4 convert_element_type.165
  113.7 1.7 copy-done.56
  115.4 1.4 fusion.96
  117.1 1.4 fusion.97
  118.6 3.8 multiply_convert_fusion
  124.0 2.0 fusion.63
  127.0 2.3 fusion.64
  129.5 2.0 broadcast_in_dim.89
  131.5 42.2 %while.51 = (s32[]{:T(128)}, f32[1,512,3,3,64]{1,4,3,2,0:T(8,128)S(1)}, bf16[1,4096,384]{1,2,0:T(8,128)(2,1)}, s32[]{:T(128)}, bf16[1,4096,384]{1,2,0:T(8,128)(2...) while((s32[]{:T(128)}, ...), condition=%wide.region_16.17_spmd.clone, body=%wide.region_13.0_spmd.clone.sunk | while | flops 3070166528 | bytes 140335616 | solution.py:52
  131.7 42.0 %conditional.11 = ((f32[1,512,3,3,64]{1,4,3,2,0:T(8,128)S(1)}, bf16[1,4096,384]{1,2,0:T(8,128)(2,1)})) conditional(s32[]{:T(128)} %convert_element_type.296, (f32[1,512,3,3,64]{1,4,3,2,0:T(8,128)S(1)}, bf16[1,4096,384]{1,2,0:T(8,128)(2,1)}) %tuple.161, (s32[]{:T(128)}, bf16[1,4096,384]{1,2,0:T(8,128)(2,1)}, s32[]{:T(128)}, ...), branch_computations={%region_14.14_spmd, %region_15.15_spmd} | conditional | flops 3070166528 | bytes 140333312 | solution.py:45
  133.0 7.9 %fusion.44 = f32[3,1024,512,3]{2,1,3,0:T(8,128)} fusion(bf16[1024,3,64,1]{0,2,3,1:T(8,128)(2,1)S(1)} %bitcast.287, bf16[1,512,3,3,64]{1,4,3,2,0:T(8,128)(2,1)S(1)} %get-tuple-element.637), kind=kOutput, calls=%fused_computation.53 | convolution fusion | flops 603979776 | bytes 19857408 | tf_op jit(solution)/shard_map/while/body/eval_jaxpr/cond/branch_1_fun/sqkgd,stkd->skgqt/dot_general | solution.py:63
  141.3 10.0 %fusion.34 = bf16[3,3,512,1024]{2,3,1,0:T(8,128)(2,1)S(1)} fusion(f32[3,1024,512,3]{2,1,3,0:T(8,128)} %fusion.44, f32[3,3,512]{2,1,0:T(4,128)S(1)} %bitcast.315, f32[3,3,512]{2,1,0:T(4,128)S(1)} %bitcast.318, pred[512,1024]{0,1:T(8,128)(4,1)S(1)} %broadcast_compare_fusion.2, bf16[1024,3,64,1]{0,2,3,1:T(8,128)(2,1)S(1)} %bitcast.294, ...), kind=kOutput, calls=%fused_computation.40 | convolution fusion | flops 632291328 | bytes 29855744 | tf_op jit(solution)/shard_map/while/body/eval_jaxpr/cond/branch_1_fun/sqkgd,stkd->skgqt/dot_general | solution.py:198
  151.3 1.8 fusion.39
  153.1 1.8 copy-done.1
  154.9 11.1 %fusion.35 = bf16[3,1024,64,1]{1,2,3,0:T(8,128)(2,1)} fusion(f32[3,1024,512,3]{2,1,3,0:T(8,128)} %fusion.44, f32[3,3,512]{2,1,0:T(4,128)} %bitcast.317, pred[512,1024]{0,1:T(8,128)(4,1)} %copy-done.4, bf16[1,512,3,3,64]{1,4,3,2,0:T(8,128)(2,1)} %get-tuple-element.639), kind=kOutput, calls=%fused_computation.41 | convolution fusion | flops 622854144 | bytes 20400128 | tf_op jit(solution)/shard_map/while/body/eval_jaxpr/cond/branch_1_fun/skgqt,sqkgd->stkd/dot_general | solution.py:212
  166.0 6.7 fusion.40
  176.1 1.8 fusion.73
  177.9 1.8 fusion.84
  179.7 2.9 fusion.100
  182.5 2.9 fusion.101
  185.4 2.9 fusion.80
  188.3 275.3 %reduce-scatter.2.cloned.1.call-done = bf16[1,512,384]{1,2,0:T(8,128)(2,1)} async-done(((bf16[1,4096,384]{1,2,0:T(8,128)(2,1)}), bf16[1,512,384]{1,2,0:T(8,128)(2,1)}) %reduce-scatter.2.cloned.1.call-update) | async-done | bytes 393232 | tf_op jit(solution)/shard_map/reduce_scatter | solution.py:243
  466.3 1.2 fusion.78
  467.6 1.2 fusion.75
  468.9 3.7 fusion.53
  474.1 2.4 fusion.61
  476.5 41.7 %all-reduce = (f32[576]{0:T(1024)}, f32[576]{0:T(1024)}) all-reduce(f32[576]{0:T(1024)S(1)} %get-tuple-element.748, f32[576]{0:T(1024)} %get-tuple-element.746), channel_id=1, replica_groups=mesh['seq'=4,'blk'=8] {'seq','blk'}, use_global_device_ids=true, to_apply=%region_27.28 | all-reduce | flops 1152 | bytes 9216 | tf_op jit(solution)/shard_map/psum | solution.py:272
  518.8 2.6 fusion.58
  521.4 209.8 %all-reduce.4.cloned.1.call-done = (f32[576,576]{1,0:T(8,128)}, f32[576,192]{0,1:T(8,128)}, f32[576,192]{0,1:T(8,128)}, f32[576,576]{1,0:T(8,128)}, f32[576,1536...) async-done(((f32[576,576]{1,0:T(8,128)}, f32[576,192]{0,1:T(8,128)}, f32[576,192]{0,1:T(8,128)}, f32[576,576]{1,0:T(8,128)}, f32[576,1536]{1,0:T(8,128)}, ...) | async-done | bytes 14155792 | tf_op jit(solution)/shard_map/psum | solution.py:272
  731.2 2.7 copy.101
  737.5 1.8 copy.105
  739.3 1.5 copy-done.15
  740.8 1.8 copy.106
  742.6 1.5 copy-done.14
  744.0 1.8 copy.107
  (190 shorter events, 25.6 us)
Async XLA Ops:
  7.2 111.4 %copy-start = (bf16[1536,576]{0,1:T(8,128)(2,1)S(1)}, bf16[1536,576]{0,1:T(8,128)(2,1)}, u32[]{:S(2)}) copy-start(bf16[1536,576]{0,1:T(8,128)(2,1)} %param.40) | copy-start | bytes 5308420
  7.2 3.6 copy-start.6
  7.2 3.6 copy-start.42
  7.2 3.6 copy-start.39
  7.2 71.8 %all-gather.2.cloned.1.call-start = ((), (), s32[]{:S(2)}) async-start(), calls=%async_computation.1 | async-start | bytes 3538944 | tf_op jit(solution)/shard_map/all_gather | solution.py:146
  8.7 2.6 copy-start.53
  9.2 7.1 copy-start.44
  11.3 1.9 copy-start.19
  12.2 5.9 copy-start.25
  12.3 3.4 copy-start.55
  13.1 450.5 %reduce-scatter.2.cloned.1.call-start = ((), (), s32[]{:S(2)}) async-start(), calls=%async_computation.2 | async-start | bytes 3538944 | tf_op jit(solution)/shard_map/reduce_scatter | solution.py:243
  20.1 105.9 %copy-start.46 = (f32[1,512]{1,0:T(1,128)}, f32[1,512]{1,0:T(1,128)S(1)}, u32[]{:S(2)}) copy-start(f32[1,512]{1,0:T(1,128)S(1)} %compare_select_fusion) | copy-start | bytes 6148
  111.1 2.4 copy-start.49
  113.5 12.4 %copy-start.13 = (f32[1,512,576]{1,2,0:T(8,128)}, f32[1,512,576]{1,2,0:T(8,128)S(1)}, u32[]{:S(2)}) copy-start(f32[1,512,576]{1,2,0:T(8,128)S(1)} %get-tuple-element.834) | copy-start | bytes 3538948
  113.5 1.9 copy-start.56
  115.4 1.7 copy-start.57
  122.3 1.7 copy-start.26
  126.3 3.0 copy-start.2
  127.0 2.3 copy-start.23
  132.9 8.3 %copy-start.24 = (bf16[1,512,3,3,64]{1,4,3,2,0:T(8,128)(2,1)S(1)}, bf16[1,512,3,3,64]{1,4,3,2,0:T(8,128)(2,1)}, u32[]{:S(2)}) copy-start(bf16[1,512,3,3,64]{1,4,3,2,0:T(8,128)(2,1)} %get-tuple-element.639) | copy-start | bytes 1769476 | tf_op jit(solution)/shard_map/while/body/eval_jaxpr/cond
  132.9 8.3 %copy-start.48 = (f32[1,3,3,512]{3,2,1,0:T(4,128)S(1)}, f32[1,3,3,512]{3,2,1,0:T(4,128)}, u32[]{:S(2)}) copy-start(f32[1,3,3,512]{3,2,1,0:T(4,128)} %get-tuple-element.640) | copy-start | bytes 55300 | tf_op jit(solution)/shard_map/while/body/eval_jaxpr/cond
  132.9 8.3 %copy-start.50 = (f32[1,3,3,512]{3,2,1,0:T(4,128)S(1)}, f32[1,3,3,512]{3,2,1,0:T(4,128)}, u32[]{:S(2)}) copy-start(f32[1,3,3,512]{3,2,1,0:T(4,128)} %get-tuple-element.638) | copy-start | bytes 55300 | tf_op jit(solution)/shard_map/while/body/eval_jaxpr/cond
  141.2 10.1 %copy-start.4 = (pred[512,1024]{0,1:T(8,128)(4,1)}, pred[512,1024]{0,1:T(8,128)(4,1)S(1)}, u32[]{:S(2)}) copy-start(pred[512,1024]{0,1:T(8,128)(4,1)S(1)} %broadcast_compare_fusion.2) | copy-start | bytes 1572868 | tf_op jit(solution)/shard_map/while/body/eval_jaxpr/cond
  151.3 3.6 copy-start.1
  166.0 6.7 copy-start.5
  173.7 557.5 %all-reduce.4.cloned.1.call-start = ((), (), s32[]{:S(2)}) async-start(), calls=%async_computation.3 | async-start | bytes 29097984 | tf_op jit(solution)/shard_map/psum | solution.py:272
  174.0 2.0 copy-start.8
  174.1 2.0 copy-start.43
  174.1 2.0 copy-start.45
  175.3 2.6 copy-start.3
  175.3 2.6 copy-start.22
  177.9 1.8 copy-start.10
  177.9 1.8 copy-start.29
  179.7 2.9 copy-start.27
  182.5 2.9 copy-start.18
  182.5 2.9 copy-start.30
  182.5 2.9 copy-start.47
  464.6 3.0 copy-start.37
  468.8 3.8 copy-start.33
  468.8 3.8 copy-start.40
  468.9 4.2 copy-start.38
  474.1 44.8 %copy-start.52 = (f32[512]{0:T(512)S(1)}, f32[512]{0:T(512)}, u32[]{:S(2)}) copy-start(f32[512]{0:T(512)} %get-tuple-element.827) | copy-start | bytes 6148
  731.2 2.7 copy-start.36
  731.2 3.5 copy-start.35
  731.2 4.3 copy-start.31
  734.8 2.7 copy-start.16
  737.5 3.3 copy-start.15
  740.7 3.3 copy-start.14
  (13 other events, 14.7 us)
Sparse Core Ops, SparseCore 0:
  13.3 65.7 all-gather.1
  173.9 289.7 reduce-scatter.1
  471.2 259.9 all-reduce.3
where the time goes:
time: 761 us; the launch traced here: 753 us
  waiting for transfers between devices  544 us (71%)
  matrix products  89.7 us (12%)
  blocking collectives  41.7 us (5%)
  local copies, waits for them, and re-layouts  32 us (4%)
  other arithmetic  27.9 us (4%)
  between operations  16.1 us (2%)
    reduce_scatter x1, waiting for transfers between devices, body(): lax.psum_scatter(term.astype(jnp.bfloat16), 'blk', scatter_dimension=1, t...  275 us
    psum x1, waiting for transfers between devices, body(): lax.psum((query_grad, key_grad, value_grad, output_grad, gate_grad, up_gr...  210 us
    all_gather x1, waiting for transfers between devices, body(): lax.all_gather(key_vals, 'blk', axis=1, tiled=True)  58.9 us
    psum x1, blocking collectives, body(): lax.psum((query_grad, key_grad, value_grad, output_grad, gate_grad, up_gr...  41.7 us
    unnamed x112, local copies, waits for them, and re-layouts  21.1 us
    dot_general x2, matrix products, block_scores(): jnp.einsum('sqkgd,stkd->skgqt', query_heads, key_heads, preferred_element...  16 us
  transfers between devices with their start and end apart: 3, of which 3 were waited for; matrix products, arithmetic and copies ran while one was open for 4% of the time, Pallas kernels for 0%

commit v1 on v0

v1 whole, which is shorter than its diff:
```python
import functools

import jax
import jax.numpy as jnp
from jax import lax
from jax.experimental import pallas as pl
from jax.experimental.pallas import tpu as pltpu
from jax.sharding import PartitionSpec as P

H = 9
KVH = 3
HD = 64
GROUP = H // KVH
HALF = HD // 2
PAIR = 2 * HD

EPSILON = 1e-05
ROPE_BASE = 100000.0
MASKED = -1e30
LOG2E = 1.4426950408889634
LN2 = 0.6931471805599453
F32 = jnp.float32
BF16 = jnp.bfloat16
VMEM_LIMIT = 56 * 1024 * 1024


def nn(a, b):
    return lax.dot_general(a, b, (((1,), (0,)), ((), ())), preferred_element_type=F32)


def nt(a, b):
    return lax.dot_general(a, b, (((1,), (1,)), ((), ())), preferred_element_type=F32)


def inverse_rms(values):
    return lax.rsqrt(jnp.mean(values * values, axis=-1, keepdims=True) + EPSILON)


def turn(rows, cos, sin):
    u, w = rows[:HALF], rows[HALF:]
    return jnp.concatenate([u * cos - w * sin, w * cos + u * sin], axis=0)


def project(tokens, gain, wq, wk, wv, cos, sin, queries, kv):
    x = tokens[...].astype(F32)
    normed = (x * inverse_rms(x) * gain[...]).astype(BF16)
    c, s = cos[...], sin[...]
    keys = nt(wk[...].T, normed)
    vals = nt(wv[...].T, normed)
    for g in range(KVH):
        kv[g * PAIR : g * PAIR + HD, :] = turn(keys[g * HD : (g + 1) * HD], c, s).astype(BF16)
        kv[g * PAIR + HD : (g + 1) * PAIR, :] = vals[g * HD : (g + 1) * HD].astype(BF16)
    raw = nt(wq[...].T, normed)
    factor = HD**-0.5 * LOG2E
    for h in range(H):
        turned = turn(raw[h * HD : (h + 1) * HD], c, s) * factor
        queries[h // GROUP, h % GROUP, :HD, :] = turned.astype(BF16)
        queries[h // GROUP, h % GROUP, HD:, :] = jnp.zeros((HD, x.shape[0]), BF16)


def first_block(queries, kv, out, top, total):
    rows = queries.shape[-1]
    part = rows // 2

    def one_group(g, carry):
        packed = kv[pl.ds(pl.multiple_of(g * PAIR, PAIR), PAIR), :]
        natural = packed.T
        for r in range(GROUP):
            for c in range(2):
                seen = (c + 1) * part
                cols = slice(c * part, seen)
                scores = nn(natural[:seen], queries[g, r, :, cols])
                key_at = lax.broadcasted_iota(jnp.int32, scores.shape, 0)
                query_at = lax.broadcasted_iota(jnp.int32, scores.shape, 1) + c * part
                scores = jnp.where(key_at <= query_at, scores, MASKED)
                high = jnp.max(scores, axis=0, keepdims=True)
                probs = jnp.exp2(scores - high)
                top[g, r, :, cols] = high
                total[g, r, :, cols] = jnp.sum(probs, axis=0, keepdims=True)
                out[g, r, :, cols] = nn(packed[HD:, :seen], probs.astype(BF16))
        return carry

    lax.fori_loop(0, KVH, one_group, 0)


def next_block(queries, kv, out, top, total):
    rows = queries.shape[-1]
    part = rows // 2

    def one_group(g, carry):
        packed = kv[pl.ds(pl.multiple_of(g * PAIR, PAIR), PAIR), :]
        natural = packed.T
        for r in range(GROUP):
            for c in range(2):
                cols = slice(c * part, (c + 1) * part)
                scores = nn(natural, queries[g, r, :, cols])
                old = top[g, r, :, cols]
                high = jnp.maximum(old, jnp.max(scores, axis=0, keepdims=True))
                probs = jnp.exp2(scores - high)
                fade = jnp.exp2(old - high)
                top[g, r, :, cols] = high
                total[g, r, :, cols] = total[g, r, :, cols] * fade + jnp.sum(
                    probs, axis=0, keepdims=True
                )
                out[g, r, :, cols] = out[g, r, :, cols] * fade + nn(
                    packed[HD:], probs.astype(BF16)
                )
        return carry

    lax.fori_loop(0, KVH, one_group, 0)


def finish_forward(out, top, total, mixed_t, lse):
    for h in range(H):
        g, r = h // GROUP, h % GROUP
        scaled = out[g, r] / total[g, r]
        out[g, r] = scaled
        mixed_t[h * HD : (h + 1) * HD, :] = scaled.astype(BF16)
        lse[g, r] = top[g, r] + jnp.log2(total[g, r])


def feed_forward(
    tokens, seed_scale, scale, wo, wg, wu, wd, gain2, cotangent, mixed_t, attended,
    layer_out, d_hidden, gate_grad, up_grad, down_grad, output_grad, gain2_grad,
    d_out, d_out_t, delta, d_normed2, down,
):
    bs = scale[0, 0]
    x = tokens[...].astype(F32)
    mixed = mixed_t[...].T
    hidden = x + bs * nn(mixed, wo[...])
    r2 = inverse_rms(hidden)
    normed2 = (hidden * r2 * gain2[...]).astype(BF16)
    normed2_t = normed2.T
    seed = cotangent[...].astype(F32) * seed_scale[...]
    d_down = (bs * seed).astype(BF16)
    ff = wg.shape[1]
    step = 512
    down[...] = jnp.zeros_like(down)
    d_normed2[...] = jnp.zeros_like(d_normed2)

    def chunk(f, carry):
        at = pl.ds(pl.multiple_of(f * step, step), step)
        gate = nn(normed2, wg[:, at])
        up = nn(normed2, wu[:, at])
        sig = 1.0 / (1.0 + jnp.exp(-gate))
        silu = gate * sig
        act = (silu * up).astype(BF16)
        d_act = nt(d_down, wd[at, :])
        d_gate = (d_act * up * (sig * (1.0 + gate * (1.0 - sig)))).astype(BF16)
        d_up = (d_act * silu).astype(BF16)
        down_grad[at, :] = nn(act.T, d_down).astype(down_grad.dtype)
        gate_grad[:, at] = nn(normed2_t, d_gate).astype(gate_grad.dtype)
        up_grad[:, at] = nn(normed2_t, d_up).astype(up_grad.dtype)
        down[...] += nn(act, wd[at, :])
        d_normed2[...] += nt(d_gate, wg[:, at]) + nt(d_up, wu[:, at])
        return carry

    lax.fori_loop(0, ff // step, chunk, 0)
    layer_out[...] = (hidden + bs * down[...]).astype(BF16)
    dn = d_normed2[...]
    gain2_grad[...] = jnp.sum(dn * hidden * r2, axis=0, keepdims=True)
    gained = gain2[...] * dn
    dh = seed + r2 * gained - hidden * (r2 * r2 * r2) * jnp.mean(gained * hidden, axis=-1, keepdims=True)
    d_hidden[...] = dh
    d_branch = (bs * dh).astype(BF16)
    output_grad[...] = nn(mixed_t[...], d_branch).astype(output_grad.dtype)
    d_mixed_t = nt(wo[...], d_branch).astype(BF16)
    rows = x.shape[0]
    for h in range(H):
        g, r = h // GROUP, h % GROUP
        head = d_mixed_t[h * HD : (h + 1) * HD]
        d_out_t[g, r, :HD, :] = jnp.zeros((HD, rows), BF16)
        d_out_t[g, r, HD:, :] = head
        d_out[g, r] = d_out_t[g, r].T
        delta[g, r] = jnp.sum(head.astype(F32) * attended[g, r], axis=0, keepdims=True)


def block_grads(queries, natural_q, d_out_t, d_out, lse, delta, kv, dq, store, masked):
    rows = queries.shape[-1]
    part = rows // 2

    def one_group(g, carry):
        packed = kv[pl.ds(pl.multiple_of(g * PAIR, PAIR), PAIR), :]
        natural = packed.T
        acc = None
        for r in range(GROUP):
            pieces = []
            for c in range(2):
                cols = slice(c * part, (c + 1) * part)
                scores = nn(natural, queries[g, r, :, cols])
                probs = jnp.exp2(scores - lse[g, r, :, cols])
                if masked:
                    key_at = lax.broadcasted_iota(jnp.int32, scores.shape, 0)
                    query_at = lax.broadcasted_iota(jnp.int32, scores.shape, 1) + c * part
                    probs = jnp.where(key_at <= query_at, probs, 0.0)
                d_probs = nn(natural, d_out_t[g, r, :, cols])
                d_scores = (probs * (d_probs - delta[g, r, :, cols])).astype(BF16)
                dq[g, r, :, cols] += nn(packed[:HD], d_scores)
                term = nn(probs.astype(BF16), d_out[g, r, cols, :]) + nn(
                    d_scores, natural_q[g, r, cols, :]
                )
                acc = term if acc is None else acc + term
        store(g, acc)
        return carry

    lax.fori_loop(0, KVH, one_group, 0)


def finish(
    tokens, gain, wq, wk, wv, cos, sin, dq, d_kv, d_hidden,
    input_grad, query_grad, key_grad, value_grad, gain_grad, turned,
):
    x = tokens[...].astype(F32)
    r1 = inverse_rms(x)
    normed_t = (x * r1 * gain[...]).astype(BF16).T
    c, s = cos[...], -sin[...]
    nq, nk = H * HD, KVH * HD
    for h in range(H):
        rows = dq[h // GROUP, h % GROUP] * HD**-0.5
        turned[h * HD : (h + 1) * HD, :] = turn(rows, c, s).astype(BF16)
    for g in range(KVH):
        both = d_kv[g].T
        turned[nq + g * HD : nq + (g + 1) * HD, :] = turn(both[:HD] * LN2, c, s).astype(BF16)
        turned[nq + nk + g * HD : nq + nk + (g + 1) * HD, :] = both[HD:].astype(BF16)
    d_normed_t = (
        nn(wq[...], turned[:nq, :])
        + nn(wk[...], turned[nq : nq + nk, :])
        + nn(wv[...], turned[nq + nk :, :])
    )
    query_grad[...] = nt(normed_t, turned[:nq, :]).astype(query_grad.dtype)
    key_grad[...] = nt(normed_t, turned[nq : nq + nk, :]).astype(key_grad.dtype)
    value_grad[...] = nt(normed_t, turned[nq + nk :, :]).astype(value_grad.dtype)
    d_normed = d_normed_t.T
    gain_grad[...] = jnp.sum(d_normed * x * r1, axis=0, keepdims=True)
    gained = gain[...] * d_normed
    input_grad[...] = (
        d_hidden[...] + r1 * gained - x * (r1 * r1 * r1) * jnp.mean(gained * x, axis=-1, keepdims=True)
    )


def project_kernel(tokens, gain, wq, wk, wv, cos, sin, queries, kv):
    project(tokens, gain, wq, wk, wv, cos, sin, queries, kv)


def forward_kernel(queries, kv_all, attended, mixed_t, lse, top, total):
    me = lax.axis_index("blk")
    first_block(queries, kv_all.at[me], attended, top, total)

    def step(i, carry):
        next_block(queries, kv_all.at[me - 1 - i], attended, top, total)
        return carry

    lax.fori_loop(0, me, step, 0)
    finish_forward(attended, top, total, mixed_t, lse)


def backward_kernel(queries, kv_all, d_out_t, d_out, lse, delta, dq, d_kv, natural_q):
    me = lax.axis_index("blk")
    dq[...] = jnp.zeros_like(dq)
    d_kv[...] = jnp.zeros_like(d_kv)
    for h in range(H):
        natural_q[h // GROUP, h % GROUP] = queries[h // GROUP, h % GROUP].T

    def run(j, masked):
        def store(g, value):
            d_kv[j, g] = value.astype(d_kv.dtype)

        block_grads(
            queries, natural_q, d_out_t, d_out, lse, delta, kv_all.at[j], dq, store, masked
        )

    def step(j, carry):
        run(j, False)
        return carry

    lax.fori_loop(0, me, step, 0)
    run(me, True)


def call(kernel, outs, scratch=(), smem=()):
    def run(*args):
        return pl.pallas_call(
            kernel,
            out_shape=[jax.ShapeDtypeStruct(s, t) for s, t in outs],
            in_specs=[
                pl.BlockSpec(memory_space=pltpu.SMEM if i in smem else pltpu.VMEM)
                for i in range(len(args))
            ],
            out_specs=[pl.BlockSpec(memory_space=pltpu.VMEM)] * len(outs),
            scratch_shapes=[pltpu.VMEM(s, t) for s, t in scratch],
            compiler_params=pltpu.CompilerParams(vmem_limit_bytes=VMEM_LIMIT),
        )(*args)

    return run


def body(blocks, tokens, positions, groups, keep_mask, exit_scales, keep_rate, wq, wk, wv, wo, wg, wu, wd, gain1, gain2, cotangent):
    tokens, cotangent = tokens[0], cotangent[0]
    rows, width = tokens.shape
    ff = wg.shape[1]
    nq, nk = H * HD, KVH * HD
    frequency = 1.0 / ROPE_BASE ** (jnp.arange(HALF, dtype=F32) * (2.0 / HD))
    angle = frequency[:, None] * positions[0].astype(F32)[None, :]
    cos, sin = jnp.cos(angle), jnp.sin(angle)
    seed_scale = jnp.where(groups[0] == 1, exit_scales[1], exit_scales[0])[:, None]
    scale = (keep_mask.astype(F32) * keep_rate)[None, :]
    gain1, gain2 = gain1[None, :], gain2[None, :]

    head_t = (KVH, GROUP, PAIR, rows)
    head_n = (KVH, GROUP, rows, PAIR)
    head_o = (KVH, GROUP, HD, rows)
    head_1 = (KVH, GROUP, 1, rows)
    queries, kv = call(project_kernel, [(head_t, BF16), ((KVH * PAIR, rows), BF16)])(
        tokens, gain1, wq, wk, wv, cos, sin
    )
    kv_all = lax.all_gather(kv, "blk", axis=0)
    attended, mixed_t, lse = call(
        forward_kernel,
        [(head_o, F32), ((nq, rows), BF16), (head_1, F32)],
        [(head_1, F32), (head_1, F32)],
    )(queries, kv_all)
    (layer_out, d_hidden, gate_grad, up_grad, down_grad, output_grad, gain2_grad, d_out, d_out_t, delta) = call(
        feed_forward,
        [
            ((rows, width), BF16),
            ((rows, width), F32),
            ((width, ff), BF16),
            ((width, ff), BF16),
            ((ff, width), BF16),
            ((nq, width), BF16),
            ((1, width), F32),
            (head_n, BF16),
            (head_t, BF16),
            (head_1, F32),
        ],
        [((rows, width), F32), ((rows, width), F32)],
        smem=(2,),
    )(tokens, seed_scale, scale, wo, wg, wu, wd, gain2, cotangent, mixed_t, attended)
    early = lax.psum((gate_grad, up_grad, down_grad, output_grad), ("seq", "blk"))
    dq, d_kv = call(
        backward_kernel,
        [(head_o, F32), ((blocks, KVH, rows, PAIR), BF16)],
        [(head_n, BF16)],
    )(queries, kv_all, d_out_t, d_out, lse, delta)
    d_kv = lax.psum_scatter(d_kv, "blk", scatter_dimension=0, tiled=False).astype(F32)
    input_grad, query_grad, key_grad, value_grad, gain1_grad = call(
        finish,
        [
            ((rows, width), F32),
            ((width, nq), BF16),
            ((width, nk), BF16),
            ((width, nk), BF16),
            ((1, width), F32),
        ],
        [((nq + 2 * nk, rows), BF16)],
    )(tokens, gain1, wq, wk, wv, cos, sin, dq, d_kv, d_hidden)
    late = lax.psum((query_grad, key_grad, value_grad), ("seq", "blk"))
    gains = lax.psum(jnp.concatenate([gain1_grad, gain2_grad], axis=0), ("seq", "blk"))
    return (
        layer_out[None],
        input_grad[None],
        late[0].astype(F32),
        late[1].astype(F32),
        late[2].astype(F32),
        early[3].astype(F32),
        early[0].astype(F32),
        early[1].astype(F32),
        early[2].astype(F32),
        gains[0],
        gains[1],
    )


def solution(mesh):
    local = P("seq", "blk", None)
    pair = P("seq", "blk")
    placed = (local, pair, pair, P("seq")) + (P(),) * 11 + (local,)
    return jax.shard_map(
        functools.partial(body, mesh.shape["blk"]),
        mesh=mesh,
        in_specs=placed,
        out_specs=(local, local) + (P(),) * 9,
        check_vma=False,
    )
```

time: 761 us -> 511 us (0.67); the launches traced: 753 us -> 510 us
  waiting for transfers between devices: 544 us -> 363 us
  matrix products: 89.7 us -> 0 us
  Pallas kernels: 0 us -> 53.9 us
  other arithmetic: 27.9 us -> 13.4 us
  local copies, waits for them, and re-layouts: 32 us -> 23.1 us
    reduce_scatter x1, waiting for transfers between devices: 275 us -> 180 us  [body(): lax.psum_scatter(d_kv, 'blk', scatter_dimension=0, tiled=False).astype(F32)]
    dot_general x28 -> x0, matrix products: 89.7 us -> none  [the longest x2 16 us: block_scores(): jnp.einsum('sqkgd,stkd->skgqt', query_heads, key_heads, preferred_element...]
    psum x1, waiting for transfers between devices: 210 us -> 128 us  [body(): late = lax.psum((query_grad, key_grad, value_grad), ('seq', 'blk'))]
    pallas_call x0 -> x5, Pallas kernels: none -> 53.9 us  [run(): pl.pallas_call(kernel, out_shape=[jax.ShapeDtypeStruct(s, t) for s, t in...]
    reduce_sum x2 -> x0, other arithmetic: 12.2 us -> none  [the longest x1 10.8 us: stats_work(): jnp.sum(jnp.where(causal, jnp.exp(scores - new_max[..., None]), 0.0), axi...]
    convert_element_type x4 -> x6, other arithmetic: 1.51 us -> 11.2 us  [the longest x1 3.87 us: body(): early[0].astype(F32)]
    unnamed x112 -> x36, local copies, waits for them, and re-layouts: 21.1 us -> 19.2 us
  transfers between devices with their start and end apart: 3 -> 3, of which waited for: 3 -> 3; matrix products, arithmetic and copies ran while one was open for 4% -> 2% of each run, Pallas kernels for 0% -> 0%
where the time goes in v1:
time: 511 us; the launch traced here: 510 us
  waiting for transfers between devices  363 us (71%)
  Pallas kernels  53.9 us (11%)
  blocking collectives  41.5 us (8%)
  local copies, waits for them, and re-layouts  23.1 us (5%)
  between operations  15.1 us (3%)
  other arithmetic  13.4 us (3%)
    reduce_scatter x1, waiting for transfers between devices, body(): lax.psum_scatter(d_kv, 'blk', scatter_dimension=0, tiled=False).astype(F32)  180 us
    psum x1, waiting for transfers between devices, body(): late = lax.psum((query_grad, key_grad, value_grad), ('seq', 'blk'))  128 us
    all_gather x1, waiting for transfers between devices, body(): kv_all = lax.all_gather(kv, 'blk', axis=0)  55.3 us
    pallas_call x5, Pallas kernels, run(): pl.pallas_call(kernel, out_shape=[jax.ShapeDtypeStruct(s, t) for s, t in...  53.9 us
    psum x1, blocking collectives, body(): lax.psum(jnp.concatenate([gain1_grad, gain2_grad], axis=0), ('seq', 'blk'))  41.5 us
    unnamed x36, local copies, waits for them, and re-layouts  19.2 us
  transfers between devices with their start and end apart: 3, of which 3 were waited for; matrix products, arithmetic and copies ran while one was open for 2% of the time, Pallas kernels for 0%

profile of v1, /device:TPU:0, one launch (start us, length us, event | category | flops | bytes accessed | tf_op | source)
XLA Modules:
  0.0 510.5 jit_solution(11573973743730956164)
XLA Ops:
  7.2 0.0 all-gather.3.cloned.1.call-start
  7.2 0.7 convert_element_type.34
  7.9 1.3 broadcast_in_dim.30.gain
  9.2 1.8 copy.41.wk
  11.0 1.8 copy.42.wv
  12.8 2.2 copy.39
  15.0 1.0 multiply_sine_fusion
  16.0 4.0 shard_map.239
  19.9 0.0 all-gather.3.cloned.1.call-update
  20.0 0.0 reduce-scatter.2.cloned.1.call-start
  21.3 0.0 copy-done.8
  21.3 0.6 broadcast_in_dim.29.gain2
  21.9 0.0 copy-done.12
  21.9 0.6 fusion.1
  22.5 0.0 copy-done.11
  22.5 1.3 fusion
  23.8 0.9 copy.43.seed_scale
  24.7 0.0 copy-done.7
  24.7 1.1 copy.40
  25.8 0.0 copy-done.1
  25.8 2.2 copy.44.wd
  28.0 55.3 %all-gather.3.cloned.1.call-done = bf16[3072,512]{1,0:T(8,128)(2,1)} async-done(((bf16[384,512]{1,0:T(8,128)(2,1)}), bf16[3072,512]{1,0:T(8,128)(2,1)}) %all-gather.3.cloned.1.call-update) | async-done | bytes 3145744 | tf_op jit(solution)/shard_map/all_gather | solution.py:316
  83.3 9.3 %shard_map.240 = (f32[3,3,64,512]{3,2,1,0:T(8,128)}, bf16[576,512]{1,0:T(8,128)(2,1)}, f32[3,3,1,512]{3,2,1,0:T(1,128)}) custom-call(bf16[3,3,128,512]{3,2,1,0:T(8,128)(2,1)} %get-tuple-element.33.queries, bf16[8,384,512]{2,1,0:T(8,128)(2,1)} %bitcast.14), custom_call_target="tpu_custom_call" | custom-call | tf_op jit(solution)/shard_map/pallas_call | solution.py:282
  92.6 21.1 %shard_map.241 = (bf16[512,576]{1,0:T(8,128)(2,1)}, f32[512,576]{1,0:T(8,128)}, bf16[576,1536]{1,0:T(8,128)(2,1)}, bf16[576,1536]{1,0:T(8,128)(2,1)}, bf16[1536,...) custom-call(bf16[512,576]{1,0:T(8,128)(2,1)} %bitcast.17, ...), custom_call_target="tpu_custom_call" | custom-call | tf_op jit(solution)/shard_map/pallas_call | solution.py:282
  113.7 13.7 %shard_map.242 = (f32[3,3,64,512]{3,2,1,0:T(8,128)}, bf16[8,3,512,128]{3,2,1,0:T(8,128)(2,1)}) custom-call(bf16[3,3,128,512]{3,2,1,0:T(8,128)(2,1)} %get-tuple-element.33.queries, bf16[8,384,512]{2,1,0:T(8,128)(2,1)} %bitcast.15, bf16[3,3,128,512]{3,2,1,0:T(8,128)(2,1)} %get-tuple-element.38.d_out_t, bf16[3,3,512,128]{3,2,1,0:T(8,128)(2,1)} %get-tuple-element.39.d_out, ...), custom_call_target="tpu_custom_call" | custom-call | tf_op jit(solution)/shard_map/pallas_call | solution.py:282
  127.4 0.0 reduce-scatter.2.cloned.1.call-update
  127.4 0.3 all-reduce.3.cloned.1.call-start
  127.7 180.0 %reduce-scatter.2.cloned.1.call-done = bf16[1,3,512,128]{3,2,1,0:T(8,128)(2,1)} async-done(((bf16[8,3,512,128]{3,2,1,0:T(8,128)(2,1)}), bf16[1,3,512,128]{3,2,1,0:T(8,128)(2,1)}) %reduce-scatter.2.cloned.1.call-update) | async-done | bytes 393232 | tf_op jit(solution)/shard_map/reduce_scatter | solution.py:345
  307.7 1.9 bitcast_convert_fusion.d_kv
  309.7 5.8 %shard_map.243 = (f32[512,576]{1,0:T(8,128)}, bf16[576,576]{1,0:T(8,128)(2,1)}, bf16[576,192]{1,0:T(8,128)(2,1)}, bf16[576,192]{1,0:T(8,128)(2,1)}, f32[1,576]{1,0:T(1,128)}) custom-call(bf16[512,576]{1,0:T(8,128)(2,1)} %bitcast.18, f32[1,576]{1,0:T(1,128)} %broadcast_in_dim.30.gain, bf16[576,576]{1,0:T(8,128)(2,1)} %wq.3, bf16[576,192]{1,0:T(8,128)(2,1)} %copy.41.wk, ...), custom_call_target="tpu_custom_call" | custom-call | tf_op jit(solution)/shard_map/pallas_call | solution.py:282
  315.5 0.0 all-reduce.3.cloned.1.call-update
  315.5 1.1 copy-done.6
  316.6 1.1 copy.47
  317.6 0.0 copy-done.3
  317.6 1.4 copy.48
  319.0 0.0 copy-done.9
  319.0 0.0 copy-done.10
  319.0 41.5 %psum.63 = f32[2,576]{1,0:T(2,128)S(1)} all-reduce(f32[2,576]{1,0:T(2,128)S(1)} %pad_maximum_fusion), channel_id=1, replica_groups=mesh['seq'=4,'blk'=8] {'seq','blk'}, use_global_device_ids=true, to_apply=%region_8.9 | all-reduce | flops 1152 | bytes 9216 | tf_op jit(solution)/shard_map/psum | solution.py:358
  360.6 0.6 slice_reduce_fusion
  361.2 127.7 %all-reduce.3.cloned.1.call-done = (bf16[576,192]{1,0:T(8,128)(2,1)}, bf16[576,192]{1,0:T(8,128)(2,1)}, bf16[1536,576]{1,0:T(8,128)(2,1)}, bf16[576,576]{1,0:T(8...) async-done(((bf16[576,192]{1,0:T(8,128)(2,1)}, bf16[576,192]{1,0:T(8,128)(2,1)}, bf16[1536,576]{1,0:T(8,128)(2,1)}, ...) | async-done | bytes 7077904 | tf_op jit(solution)/shard_map/psum | solution.py:357
  488.9 2.0 copy.49
  490.9 1.9 copy.50
  492.8 1.2 convert_element_type.37
  494.0 0.0 copy-done.4
  494.0 1.2 convert_element_type.40
  495.2 2.6 copy.51
  497.8 3.9 convert_element_type.41
  501.7 2.3 convert_element_type.42
  (18 shorter events, 0.0 us)
Async XLA Ops:
  7.2 76.1 %all-gather.3.cloned.1.call-start = ((), (), s32[]{:S(2)}) async-start(), calls=%async_computation.2 | async-start | bytes 3538944 | tf_op jit(solution)/shard_map/all_gather | solution.py:316
  12.8 8.5 %copy-start.8 = (f32[576]{0:T(1024)S(1)}, f32[576]{0:T(1024)}, u32[]{:S(2)}) copy-start(f32[576]{0:T(1024)} %param.30) | copy-start | bytes 6916
  12.8 9.1 %copy-start.12 = (f32[2]{0:T(128)S(1)}, f32[2]{0:T(128)}, u32[]{:S(2)}) copy-start(f32[2]{0:T(128)} %param.20) | copy-start | bytes 28
  12.8 9.7 %copy-start.11 = (s32[1,512]{1,0:T(1,128)S(1)}, s32[1,512]{1,0:T(1,128)}, u32[]{:S(2)}) copy-start(s32[1,512]{1,0:T(1,128)} %param.18) | copy-start | bytes 6148
  15.0 9.7 %copy-start.7 = (bf16[1,512,576]{1,2,0:T(8,128)(2,1)S(1)}, bf16[1,512,576]{1,2,0:T(8,128)(2,1)}, u32[]{:S(2)}) copy-start(bf16[1,512,576]{1,2,0:T(8,128)(2,1)} %param.31) | copy-start | bytes 1769476
  15.9 9.8 %copy-start.1 = (bf16[1536,576]{0,1:T(8,128)(2,1)S(1)}, bf16[1536,576]{0,1:T(8,128)(2,1)}, u32[]{:S(2)}) copy-start(bf16[1536,576]{0,1:T(8,128)(2,1)} %param.28) | copy-start | bytes 5308420
  20.0 287.8 %reduce-scatter.2.cloned.1.call-start = ((), (), s32[]{:S(2)}) async-start(), calls=%async_computation.1 | async-start | bytes 3538944 | tf_op jit(solution)/shard_map/reduce_scatter | solution.py:345
  127.4 361.4 %all-reduce.3.cloned.1.call-start = ((), (), s32[]{:S(2)}) async-start(), calls=%async_computation.3 | async-start | bytes 15138816 | tf_op jit(solution)/shard_map/psum | solution.py:357
  315.5 1.1 copy-start.6
  315.5 2.1 copy-start.3
  316.6 2.5 copy-start.9
  316.6 2.5 copy-start.10
  488.9 3.9 copy-start.5
  488.9 5.1 %copy-start.4 = (bf16[576,576]{1,0:T(8,128)(2,1)S(1)}, bf16[576,576]{1,0:T(8,128)(2,1)}, u32[]{:S(2)}) copy-start(bf16[576,576]{1,0:T(8,128)(2,1)} %get-tuple-element.83) | copy-start | bytes 1990660
  492.8 2.4 copy-start
  497.8 3.9 copy-start.2
Sparse Core Ops, SparseCore 0:
  20.1 63.1 all-gather.2
  127.6 180.1 reduce-scatter.1
  315.6 173.1 all-reduce.2

commit v2 on v1

v2 whole, which is shorter than its diff:
```python
import functools

import jax
import jax.numpy as jnp
from jax import lax
from jax.experimental import pallas as pl
from jax.experimental.pallas import tpu as pltpu
from jax.sharding import PartitionSpec as P

H = 9
KVH = 3
HD = 64
GROUP = H // KVH
HALF = HD // 2
PAIR = 2 * HD

EPSILON = 1e-05
ROPE_BASE = 100000.0
MASKED = -1e30
LOG2E = 1.4426950408889634
LN2 = 0.6931471805599453
F32 = jnp.float32
BF16 = jnp.bfloat16
VMEM_LIMIT = 56 * 1024 * 1024
MESH = pl.DeviceIdType.MESH


def nn(a, b):
    return lax.dot_general(a, b, (((1,), (0,)), ((), ())), preferred_element_type=F32)


def nt(a, b):
    return lax.dot_general(a, b, (((1,), (1,)), ((), ())), preferred_element_type=F32)


def column(row):
    return jnp.broadcast_to(row, (8, row.shape[1])).T[:, :1]


def inverse_rms(values):
    return lax.rsqrt(jnp.mean(values * values, axis=0, keepdims=True) + EPSILON)


def turn(rows, cos, sin):
    u, w = rows[:HALF], rows[HALF:]
    return jnp.concatenate([u * cos - w * sin, w * cos + u * sin], axis=0)


def normalize(tokens, gain):
    x = tokens[...].astype(F32)
    return (x * inverse_rms(x) * column(gain[...])).astype(BF16)


def project_kv(normed, wk, wv, cos, sin, kv):
    keys = nn(wk[...], normed)
    vals = nn(wv[...], normed)
    for g in range(KVH):
        span = slice(g * HD, (g + 1) * HD)
        kv[g, :HD, :] = turn(keys[span], cos, sin).astype(BF16)
        kv[g, HD:, :] = vals[span].astype(BF16)


def project_q(normed, wq, cos, sin, queries):
    raw = nn(wq[...].T, normed)
    factor = HD**-0.5 * LOG2E
    for h in range(H):
        turned = turn(raw[h * HD : (h + 1) * HD], cos, sin) * factor
        queries[h // GROUP, h % GROUP, :HD, :] = turned.astype(BF16)
        queries[h // GROUP, h % GROUP, HD:, :] = jnp.zeros((HD, raw.shape[1]), BF16)


def values_and_ones(packed):
    ones = jnp.ones((16, packed.shape[1]), BF16)
    return jnp.concatenate([packed[HD:], ones], axis=0)


def first_unit(g, queries, packed, out, top, total):
    rows = queries.shape[-1]
    part = rows // 2
    natural = packed.T
    values = values_and_ones(packed)
    items = [(r, c) for r in range(GROUP) for c in range(2)]

    def scores_of(i):
        r, c = items[i]
        return nn(natural[: (c + 1) * part], queries[g, r, :, c * part : (c + 1) * part])

    scores = scores_of(0)
    done = []
    for i, (r, c) in enumerate(items):
        later = scores_of(i + 1) if i + 1 < len(items) else None
        key_at = lax.broadcasted_iota(jnp.int32, scores.shape, 0)
        query_at = lax.broadcasted_iota(jnp.int32, scores.shape, 1) + c * part
        scores = jnp.where(key_at <= query_at, scores, MASKED)
        high = jnp.max(scores, axis=0, keepdims=True)
        probs = jnp.exp2(scores - high)
        done.append((high, nn(values[:, : (c + 1) * part], probs.astype(BF16))))
        scores = later
    for (r, c), (high, summed) in zip(items, done):
        cols = slice(c * part, (c + 1) * part)
        top[g, r, :, cols] = high
        total[g, r, :, cols] = summed[HD : HD + 1]
        out[g, r, :, cols] = summed[:HD]


def next_unit(g, queries, packed, out, top, total):
    natural = packed.T
    values = values_and_ones(packed)
    before = [(top[g, r], total[g, r], out[g, r]) for r in range(GROUP)]
    scores = [nn(natural, queries[g, r]) for r in range(2)]
    done = []
    for r in range(GROUP):
        if r + 2 < GROUP:
            scores.append(nn(natural, queries[g, r + 2]))
        old, count, acc = before[r]
        high = jnp.maximum(old, jnp.max(scores[r], axis=0, keepdims=True))
        probs = jnp.exp2(scores[r] - high)
        fade = jnp.exp2(old - high)
        summed = nn(values, probs.astype(BF16))
        done.append((high, count * fade + summed[HD : HD + 1], acc * fade + summed[:HD]))
    for r, (high, count, acc) in enumerate(done):
        top[g, r] = high
        total[g, r] = count
        out[g, r] = acc


def finish_forward(out, top, total, mixed_t, lse):
    for h in range(H):
        g, r = h // GROUP, h % GROUP
        scaled = out[g, r] * (1.0 / total[g, r])
        out[g, r] = scaled
        mixed_t[h * HD : (h + 1) * HD, :] = scaled.astype(BF16)
        lse[g, r] = top[g, r] + jnp.log2(total[g, r])


def forward_kernel(
    blocks, tokens, gain, wq, wk, wv, cos, sin,
    queries, kv_all, attended, mixed_t, lse,
    top, total, send_sem, recv_sem,
):
    s, b = lax.axis_index("seq"), lax.axis_index("blk")
    z, y, floors = b // 2, b % 2, blocks // 2
    above, below, across = (s, b + 2), (s, b - 2), (s, b + 1 - 2 * y)
    has_above, has_below = z < floors - 1, z > 0

    barrier = pltpu.get_barrier_semaphore()
    pl.semaphore_signal(barrier, inc=1, device_id=across, device_id_type=MESH)

    @pl.when(has_above)
    def _():
        pl.semaphore_signal(barrier, inc=1, device_id=above, device_id_type=MESH)

    @pl.when(has_below)
    def _():
        pl.semaphore_signal(barrier, inc=1, device_id=below, device_id_type=MESH)

    def copy(kind, j, g):
        return pltpu.make_async_remote_copy(
            src_ref=kv_all.at[j, g],
            dst_ref=kv_all.at[j, g],
            send_sem=send_sem.at[kind, j, g],
            recv_sem=recv_sem.at[j, g],
            device_id=above if kind == 0 else across,
            device_id_type=MESH,
        )

    normed = normalize(tokens, gain)
    c, sn = cos[...], sin[...]
    project_kv(normed, wk, wv, c, sn, kv_all.at[b])
    pl.semaphore_wait(barrier, 1 + has_above.astype(jnp.int32) + has_below.astype(jnp.int32))

    def send_own(g, carry):
        @pl.when(has_above)
        def _():
            copy(0, b, g).start()

        @pl.when(y == 0)
        def _():
            copy(1, b, g).start()

        return carry

    lax.fori_loop(0, KVH, send_own, 0)
    project_q(normed, wq, c, sn, queries)

    def own(g, carry):
        first_unit(g, queries, kv_all[b, g], attended, top, total)
        return carry

    lax.fori_loop(0, KVH, own, 0)

    def level(m, carry):
        def one(g, inner):
            @pl.when(m <= z)
            def _():
                j = b - 2 * m
                copy(0, j, g).wait_recv()

                @pl.when(has_above)
                def _():
                    copy(0, j, g).start()

                copy(1, j, g).start()
                next_unit(g, queries, kv_all[j, g], attended, top, total)

            @pl.when((m >= 2) | (y == 1))
            def _():
                j = b - 2 * m + 3 - 2 * y
                copy(1, j, g).wait_recv()
                next_unit(g, queries, kv_all[j, g], attended, top, total)

            return inner

        return lax.fori_loop(0, KVH, one, carry)

    lax.fori_loop(1, z + 2, level, 0)
    finish_forward(attended, top, total, mixed_t, lse)

    def drain(m, carry):
        def one(g, inner):
            j = b - 2 * m

            @pl.when(has_above)
            def _():
                copy(0, j, g).wait_send()

            @pl.when((m >= 1) | (y == 0))
            def _():
                copy(1, j, g).wait_send()

            return inner

        return lax.fori_loop(0, KVH, one, carry)

    lax.fori_loop(0, z + 1, drain, 0)


def feed_forward(
    tokens, seed_scale, scale, wo, wg, wu, wd, gain2, cotangent, mixed_t, attended,
    layer_out, d_hidden, gate_grad, up_grad, down_grad, output_grad, gain2_grad,
    d_out, delta, d_normed2, down,
):
    bs = scale[0, 0]
    gain = column(gain2[...])
    hidden = tokens[...].astype(F32) + bs * nn(wo[...].T, mixed_t[...])
    r2 = inverse_rms(hidden)
    normed2_t = (hidden * r2 * gain).astype(BF16)
    normed2 = normed2_t.T
    seed = cotangent[...].astype(F32) * seed_scale[...]
    d_down_t = (bs * seed).astype(BF16)
    d_down = d_down_t.T
    ff = wg.shape[1]
    step = 512
    down[...] = jnp.zeros_like(down)
    d_normed2[...] = jnp.zeros_like(d_normed2)

    def chunk(f, carry):
        at = pl.ds(pl.multiple_of(f * step, step), step)
        gate = nn(normed2, wg[:, at])
        up = nn(normed2, wu[:, at])
        d_act = nn(d_down, wd[:, at])
        sig = 1.0 / (1.0 + jnp.exp(-gate))
        silu = gate * sig
        act = (silu * up).astype(BF16)
        d_gate = (d_act * up * (sig + silu * (1.0 - sig))).astype(BF16)
        d_up = (d_act * silu).astype(BF16)
        down_grad[:, at] = nn(d_down_t, act).astype(down_grad.dtype)
        gate_grad[:, at] = nn(normed2_t, d_gate).astype(gate_grad.dtype)
        up_grad[:, at] = nn(normed2_t, d_up).astype(up_grad.dtype)
        down[...] += nt(wd[:, at], act)
        d_normed2[...] += nt(wg[:, at], d_gate) + nt(wu[:, at], d_up)
        return carry

    lax.fori_loop(0, ff // step, chunk, 0)
    layer_out[...] = (hidden + bs * down[...]).astype(BF16)
    dn = d_normed2[...]
    gain2_grad[...] = jnp.sum(dn * hidden * r2, axis=1, keepdims=True)
    gained = gain * dn
    dh = seed + r2 * gained - hidden * (r2 * r2 * r2) * jnp.mean(gained * hidden, axis=0, keepdims=True)
    d_hidden[...] = dh
    d_branch = (bs * dh).astype(BF16)
    output_grad[...] = nt(mixed_t[...], d_branch).astype(output_grad.dtype)
    d_mixed = nn(wo[...], d_branch).astype(BF16)
    rows = d_mixed.shape[1]
    for h in range(H):
        g, r = h // GROUP, h % GROUP
        head = d_mixed[h * HD : (h + 1) * HD]
        d_out[g, r, :HD, :] = jnp.zeros((HD, rows), BF16)
        d_out[g, r, HD:, :] = head
        delta[g, r] = jnp.sum(head.astype(F32) * attended[g, r], axis=0, keepdims=True)


def grad_unit(g, queries, d_out, lse, delta, packed, dq, masked):
    rows = queries.shape[-1]
    natural = packed.T
    before = [dq[g, r] for r in range(GROUP)]

    def products(r):
        return nn(natural, queries[g, r]), nn(natural, d_out[g, r])

    ahead = products(0)
    done = []
    d_keys, d_vals = None, None
    for r in range(GROUP):
        scores, d_probs = ahead
        if r + 1 < GROUP:
            ahead = products(r + 1)
        probs = jnp.exp2(scores - lse[g, r])
        if masked:
            key_at = lax.broadcasted_iota(jnp.int32, scores.shape, 0)
            query_at = lax.broadcasted_iota(jnp.int32, scores.shape, 1)
            probs = jnp.where(key_at <= query_at, probs, 0.0)
        d_scores = (probs * (d_probs - delta[g, r])).astype(BF16)
        keys_term = nt(queries[g, r, :HD], d_scores)
        vals_term = nt(d_out[g, r, HD:], probs.astype(BF16))
        d_keys = keys_term if d_keys is None else d_keys + keys_term
        d_vals = vals_term if d_vals is None else d_vals + vals_term
        done.append(before[r] + nn(packed[:HD], d_scores))
    for r in range(GROUP):
        dq[g, r] = done[r]
    return d_keys * LN2, d_vals


def backward_kernel(queries, kv_all, d_out, lse, delta, dq, d_kv):
    me = lax.axis_index("blk")
    dq[...] = jnp.zeros_like(dq)
    d_kv[...] = jnp.zeros_like(d_kv)

    def run(j, masked):
        def one(g, carry):
            d_keys, d_vals = grad_unit(
                g, queries, d_out, lse, delta, kv_all[j, g], dq, masked
            )
            d_kv[j, g, :HD] = d_keys.astype(BF16)
            d_kv[j, g, HD:] = d_vals.astype(BF16)
            return carry

        lax.fori_loop(0, KVH, one, 0)

    def step(j, carry):
        run(j, False)
        return carry

    lax.fori_loop(0, me, step, 0)
    run(me, True)


def finish(
    tokens, gain, wq, wk, wv, cos, sin, dq, d_kv, d_hidden,
    input_grad, query_grad, key_grad, value_grad, gain_grad, turned,
):
    x = tokens[...].astype(F32)
    r1 = inverse_rms(x)
    weight = column(gain[...])
    normed = (x * r1 * weight).astype(BF16)
    c, s = cos[...], -sin[...]
    nq, nk = H * HD, KVH * HD
    for h in range(H):
        rows = dq[h // GROUP, h % GROUP] * HD**-0.5
        turned[h * HD : (h + 1) * HD, :] = turn(rows, c, s).astype(BF16)
    for g in range(KVH):
        turned[nq + g * HD : nq + (g + 1) * HD, :] = turn(d_kv[g, :HD], c, s).astype(BF16)
        turned[nq + nk + g * HD : nq + nk + (g + 1) * HD, :] = d_kv[g, HD:].astype(BF16)
    d_normed = (
        nn(wq[...], turned[:nq, :])
        + nn(wk[...].T, turned[nq : nq + nk, :])
        + nn(wv[...].T, turned[nq + nk :, :])
    )
    query_grad[...] = nt(normed, turned[:nq, :]).astype(query_grad.dtype)
    key_grad[...] = nt(turned[nq : nq + nk, :], normed).astype(key_grad.dtype)
    value_grad[...] = nt(turned[nq + nk :, :], normed).astype(value_grad.dtype)
    gain_grad[...] = jnp.sum(d_normed * x * r1, axis=1, keepdims=True)
    gained = weight * d_normed
    input_grad[...] = (
        d_hidden[...] + r1 * gained - x * (r1 * r1 * r1) * jnp.mean(gained * x, axis=0, keepdims=True)
    )


def call(kernel, outs, scratch=(), smem=(), **params):
    def run(*args):
        return pl.pallas_call(
            kernel,
            out_shape=[jax.ShapeDtypeStruct(s, t) for s, t in outs],
            in_specs=[
                pl.BlockSpec(memory_space=pltpu.SMEM if i in smem else pltpu.VMEM)
                for i in range(len(args))
            ],
            out_specs=[pl.BlockSpec(memory_space=pltpu.VMEM)] * len(outs),
            scratch_shapes=list(scratch),
            compiler_params=pltpu.CompilerParams(vmem_limit_bytes=VMEM_LIMIT, **params),
        )(*args)

    return run


def body(blocks, tokens, positions, groups, keep_mask, exit_scales, keep_rate, wq, wk, wv, wo, wg, wu, wd, gain1, gain2, cotangent):
    tokens, cotangent = tokens[0].T, cotangent[0].T
    wk, wv, wd = wk.T, wv.T, wd.T
    width, rows = tokens.shape
    ff = wg.shape[1]
    nq, nk = H * HD, KVH * HD
    frequency = 1.0 / ROPE_BASE ** (jnp.arange(HALF, dtype=F32) * (2.0 / HD))
    angle = frequency[:, None] * positions[0].astype(F32)[None, :]
    cos, sin = jnp.cos(angle), jnp.sin(angle)
    seed_scale = jnp.where(groups == 1, exit_scales[1], exit_scales[0])
    scale = (keep_mask.astype(F32) * keep_rate)[None, :]
    gain1, gain2 = gain1[None, :], gain2[None, :]

    head_t = (KVH, GROUP, PAIR, rows)
    head_o = (KVH, GROUP, HD, rows)
    head_1 = (KVH, GROUP, 1, rows)
    queries, kv_all, attended, mixed_t, lse = call(
        functools.partial(forward_kernel, blocks),
        [
            (head_t, BF16),
            ((blocks, KVH, PAIR, rows), BF16),
            (head_o, F32),
            ((nq, rows), BF16),
            (head_1, F32),
        ],
        [
            pltpu.VMEM(head_1, F32),
            pltpu.VMEM(head_1, F32),
            pltpu.SemaphoreType.DMA((2, blocks, KVH)),
            pltpu.SemaphoreType.DMA((blocks, KVH)),
        ],
        collective_id=0,
        has_side_effects=True,
    )(tokens, gain1, wq, wk, wv, cos, sin)
    (layer_out, d_hidden, gate_grad, up_grad, down_grad, output_grad, gain2_grad, d_out, delta) = call(
        feed_forward,
        [
            ((width, rows), BF16),
            ((width, rows), F32),
            ((width, ff), BF16),
            ((width, ff), BF16),
            ((width, ff), BF16),
            ((nq, width), BF16),
            ((width, 1), F32),
            (head_t, BF16),
            (head_1, F32),
        ],
        [pltpu.VMEM((width, rows), F32), pltpu.VMEM((width, rows), F32)],
        smem=(2,),
    )(tokens, seed_scale, scale, wo, wg, wu, wd, gain2, cotangent, mixed_t, attended)
    early = lax.psum((gate_grad, up_grad, down_grad, output_grad), ("seq", "blk"))
    dq, d_kv = call(
        backward_kernel,
        [(head_o, F32), ((blocks, KVH, PAIR, rows), BF16)],
    )(queries, kv_all, d_out, lse, delta)
    d_kv = lax.psum_scatter(d_kv, "blk", scatter_dimension=0, tiled=False).astype(F32)
    input_grad, query_grad, key_grad, value_grad, gain1_grad = call(
        finish,
        [
            ((width, rows), F32),
            ((width, nq), BF16),
            ((nk, width), BF16),
            ((nk, width), BF16),
            ((width, 1), F32),
        ],
        [pltpu.VMEM((nq + 2 * nk, rows), BF16)],
    )(tokens, gain1, wq, wk, wv, cos, sin, dq, d_kv, d_hidden)
    late = lax.psum((query_grad, key_grad, value_grad), ("seq", "blk"))
    gains = lax.psum(jnp.concatenate([gain1_grad, gain2_grad], axis=1), ("seq", "blk"))
    return (
        layer_out.T[None],
        input_grad.T[None],
        late[0].astype(F32),
        late[1].astype(F32).T,
        late[2].astype(F32).T,
        early[3].astype(F32),
        early[0].astype(F32),
        early[1].astype(F32),
        early[2].astype(F32).T,
        gains[:, 0],
        gains[:, 1],
    )


def solution(mesh):
    local = P("seq", "blk", None)
    pair = P("seq", "blk")
    placed = (local, pair, pair, P("seq")) + (P(),) * 11 + (local,)
    return jax.shard_map(
        functools.partial(body, mesh.shape["blk"]),
        mesh=mesh,
        in_specs=placed,
        out_specs=(local, local) + (P(),) * 9,
        check_vma=False,
    )
```

time: 511 us -> 410 us (0.80)
  waiting for transfers between devices: 363 us -> 276 us
  local copies, waits for them, and re-layouts: 23.1 us -> 5.69 us
  other arithmetic: 13.4 us -> 19 us
    all_gather x1 -> x0, waiting for transfers between devices: 55.3 us -> none  [body(): kv_all = lax.all_gather(kv, 'blk', axis=0)]
    reduce_scatter x1, waiting for transfers between devices: 180 us -> 149 us  [body(): lax.psum_scatter(d_kv, 'blk', scatter_dimension=0, tiled=False).astype(F32)]
    unnamed x36 -> x14, local copies, waits for them, and re-layouts: 19.2 us -> 0.95 us
    transpose x0 -> x3, other arithmetic: none -> 5.89 us  [the longest x1 2.26 us: body(): early[2].astype(F32)]
    pallas_call x5 -> x4, Pallas kernels: 53.9 us -> 52.4 us  [run(): pl.pallas_call(kernel, out_shape=[jax.ShapeDtypeStruct(s, t) for s, t in...]
  transfers between devices with their start and end apart: 3 -> 2, of which waited for: 3 -> 2; matrix products, arithmetic and copies ran while one was open for 2% -> 0% of each run, Pallas kernels for 0% -> 0%
where the time goes in v2:
time: 410 us
  waiting for transfers between devices  276 us (67%)
  Pallas kernels  52.4 us (13%)
  blocking collectives  41.6 us (10%)
  other arithmetic  19 us (5%)
  between operations  15.4 us (4%)
  local copies, waits for them, and re-layouts  5.69 us (1%)
    reduce_scatter x1, waiting for transfers between devices, body(): lax.psum_scatter(d_kv, 'blk', scatter_dimension=0, tiled=False).astype(F32)  149 us
    psum x1, waiting for transfers between devices, body(): late = lax.psum((query_grad, key_grad, value_grad), ('seq', 'blk'))  127 us
    pallas_call x4, Pallas kernels, run(): pl.pallas_call(kernel, out_shape=[jax.ShapeDtypeStruct(s, t) for s, t in...  52.4 us
    psum x1, blocking collectives, body(): lax.psum(jnp.concatenate([gain1_grad, gain2_grad], axis=1), ('seq', 'blk'))  41.6 us
  transfers between devices with their start and end apart: 2, of which 2 were waited for; matrix products, arithmetic and copies ran while one was open for 0% of the time, Pallas kernels for 0%

profile of v2, /device:TPU:0, one launch (start us, length us, event | category | flops | bytes accessed | tf_op | source)
XLA Modules:
  0.0 409.8 jit_solution(612314721223516142)
XLA Ops:
  7.2 0.0 reduce-scatter.2.cloned.1.call-start
  8.5 1.3 fusion
  9.9 0.7 convert_element_type.28
  10.5 1.3 broadcast_in_dim.29.gain
  11.8 1.3 broadcast_in_dim.28.gain2
  13.1 1.0 multiply_sine_fusion
  14.0 2.6 compare_select_fusion.seed_scale
  16.6 16.1 %shard_map.239 = (bf16[3,3,128,512]{3,2,1,0:T(8,128)(2,1)}, bf16[8,3,128,512]{3,2,1,0:T(8,128)(2,1)}, f32[3,3,64,512]{3,2,1,0:T(8,128)}, bf16[576,512]{1,0:T(8,128)(2,1)}, f32[3,3,1,512]{3,2,1,0:T(1,128)}) custom-call(bf16[576,512]{1,0:T(8,128)(2,1)} %bitcast.25, f32[1,576]{1,0:T(1,128)} %broadcast_in_dim.29.gain, bf16[576,576]{1,0:T(8,128)(2,1)} %wq.3, ...), custom_call_target="tpu_custom_call" | custom-call | tf_op jit(solution)/shard_map/pallas_call | solution.py:381
  32.7 19.4 %shard_map.240 = (bf16[576,512]{1,0:T(8,128)(2,1)}, f32[576,512]{1,0:T(8,128)}, bf16[576,1536]{1,0:T(8,128)(2,1)}, bf16[576,1536]{1,0:T(8,128)(2,1)}, bf16[576,1...) custom-call(bf16[576,512]{1,0:T(8,128)(2,1)} %bitcast.26, ...), custom_call_target="tpu_custom_call" | custom-call | tf_op jit(solution)/shard_map/pallas_call | solution.py:381
  52.1 11.0 %shard_map.241 = (f32[3,3,64,512]{3,2,1,0:T(8,128)}, bf16[8,3,128,512]{3,2,1,0:T(8,128)(2,1)}) custom-call(bf16[3,3,128,512]{3,2,1,0:T(8,128)(2,1)} %get-tuple-element.35.queries, bf16[8,3,128,512]{3,2,1,0:T(8,128)(2,1)} %get-tuple-element.36.kv_all, bf16[3,3,128,512]{3,2,1,0:T(8,128)(2,1)} %get-tuple-element.37.d_out, ...), custom_call_target="tpu_custom_call" | custom-call | tf_op jit(solution)/shard_map/pallas_call | solution.py:381
  63.1 0.0 reduce-scatter.2.cloned.1.call-update
  63.2 0.0 all-reduce.3.cloned.1.call-start
  63.2 148.8 %reduce-scatter.2.cloned.1.call-done = bf16[1,3,128,512]{3,2,1,0:T(8,128)(2,1)} async-done(((bf16[8,3,128,512]{3,2,1,0:T(8,128)(2,1)}), bf16[1,3,128,512]{3,2,1,0:T(8,128)(2,1)}) %reduce-scatter.2.cloned.1.call-update) | async-done | bytes 393232 | tf_op jit(solution)/shard_map/reduce_scatter | solution.py:451
  212.0 2.0 bitcast_convert_fusion.d_kv
  214.0 5.9 %shard_map.242 = (f32[576,512]{1,0:T(8,128)}, bf16[576,576]{1,0:T(8,128)(2,1)}, bf16[192,576]{1,0:T(8,128)(2,1)}, bf16[192,576]{1,0:T(8,128)(2,1)}, f32[576,1]{1,0:T(8,128)}) custom-call(bf16[576,512]{1,0:T(8,128)(2,1)} %bitcast.27, f32[1,576]{1,0:T(1,128)} %broadcast_in_dim.29.gain, bf16[576,576]{1,0:T(8,128)(2,1)} %wq.3, bf16[192,576]{1,0:T(8,128)(2,1)} %bitcast.31, ...), custom_call_target="tpu_custom_call" | custom-call | tf_op jit(solution)/shard_map/pallas_call | solution.py:381
  219.9 0.0 copy-start.5
  219.9 0.0 copy-start.6
  219.9 0.0 all-reduce.3.cloned.1.call-update
  219.9 0.9 copy-done.5
  220.9 0.1 copy.28
  221.0 0.0 copy-done.6
  221.0 0.2 copy.27
  221.2 41.6 %psum.63 = f32[576,2]{0,1:T(2,128)S(1)} all-reduce(f32[576,2]{0,1:T(2,128)S(1)} %pad_maximum_fusion), channel_id=1, replica_groups=mesh['seq'=4,'blk'=8] {'seq','blk'}, use_global_device_ids=true, to_apply=%region_8.9 | all-reduce | flops 1152 | bytes 9216 | tf_op jit(solution)/shard_map/psum | solution.py:464
  262.8 0.6 slice_reduce_fusion
  263.4 126.7 %all-reduce.3.cloned.1.call-done = (bf16[576,576]{1,0:T(8,128)(2,1)}, bf16[576,192]{0,1:T(8,128)(2,1)}, bf16[576,192]{0,1:T(8,128)(2,1)}, bf16[576,576]{1,0:T(8,...) async-done(((bf16[576,576]{1,0:T(8,128)(2,1)}, bf16[576,192]{0,1:T(8,128)(2,1)}, bf16[576,192]{0,1:T(8,128)(2,1)}, ...) | async-done | bytes 7077904 | tf_op jit(solution)/shard_map/psum | solution.py:463
  390.1 0.0 copy-start.4
  390.1 0.0 copy-start.3
  390.1 1.9 transpose.49
  392.0 1.8 transpose.51
  393.7 0.0 copy-done.4
  393.7 0.0 copy-start.2
  393.7 1.2 convert_element_type.31
  394.9 0.0 copy-done.3
  394.9 1.2 convert_element_type.32
  396.2 0.0 copy-done.2
  396.2 0.0 copy-start.1
  396.2 2.3 convert_element_type.33
  398.4 0.0 copy-done.1
  398.4 0.0 copy-start
  398.4 2.3 convert_element_type.34
  400.7 0.0 copy-done
  400.7 2.3 transpose.53
  (2 shorter events, 0.0 us)
Async XLA Ops:
  7.2 204.8 %reduce-scatter.2.cloned.1.call-start = ((), (), s32[]{:S(2)}) async-start(), calls=%async_computation.1 | async-start | bytes 3538944 | tf_op jit(solution)/shard_map/reduce_scatter | solution.py:451
  63.2 326.9 %all-reduce.3.cloned.1.call-start = ((), (), s32[]{:S(2)}) async-start(), calls=%async_computation.2 | async-start | bytes 14548992 | tf_op jit(solution)/shard_map/psum | solution.py:463
  219.9 1.0 copy-start.5
  219.9 1.1 copy-start.6
  390.1 3.6 copy-start.4
  390.1 4.8 %copy-start.3 = (bf16[576,576]{1,0:T(8,128)(2,1)S(1)}, bf16[576,576]{1,0:T(8,128)(2,1)}, u32[]{:S(2)}) copy-start(bf16[576,576]{1,0:T(8,128)(2,1)} %get-tuple-element.58) | copy-start | bytes 1990660
  393.7 2.4 copy-start.2
  396.2 2.3 copy-start.1
  398.4 2.3 copy-start
Sparse Core Ops, SparseCore 0:
  63.3 148.6 reduce-scatter.1
  220.0 170.0 all-reduce.2

commit v3 on v2

v3 whole, which is shorter than its diff:
```python
import functools

import jax
import jax.numpy as jnp
from jax import lax
from jax.experimental import pallas as pl
from jax.experimental.pallas import tpu as pltpu
from jax.sharding import PartitionSpec as P

H = 9
KVH = 3
HD = 64
GROUP = H // KVH
HALF = HD // 2
PAIR = 2 * HD

EPSILON = 1e-05
ROPE_BASE = 100000.0
MASKED = -1e30
LOG2E = 1.4426950408889634
LN2 = 0.6931471805599453
F32 = jnp.float32
BF16 = jnp.bfloat16
VMEM_LIMIT = 61 * 1024 * 1024
MESH = pl.DeviceIdType.MESH
LANES = 128


def nn(a, b):
    return lax.dot_general(a, b, (((1,), (0,)), ((), ())), preferred_element_type=F32)


def nt(a, b):
    return lax.dot_general(a, b, (((1,), (1,)), ((), ())), preferred_element_type=F32)


def column(row):
    return jnp.broadcast_to(row, (8, row.shape[1])).T[:, :1]


def inverse_rms(values):
    return lax.rsqrt(jnp.mean(values * values, axis=0, keepdims=True) + EPSILON)


def turn(rows, cos, sin):
    u, w = rows[:HALF], rows[HALF:]
    return jnp.concatenate([u * cos - w * sin, w * cos + u * sin], axis=0)


def normalize(tokens, gain):
    x = tokens[...].astype(F32)
    return (x * inverse_rms(x) * column(gain[...])).astype(BF16)


def project_kv(normed, wk, wv, cos, sin, kv):
    keys = nn(wk[...], normed)
    vals = nn(wv[...], normed)
    for g in range(KVH):
        span = slice(g * HD, (g + 1) * HD)
        kv[g, :HD, :] = turn(keys[span], cos, sin).astype(BF16)
        kv[g, HD:, :] = vals[span].astype(BF16)


def project_q(normed, wq, cos, sin, queries):
    raw = nn(wq[...].T, normed)
    factor = HD**-0.5 * LOG2E
    for h in range(H):
        turned = turn(raw[h * HD : (h + 1) * HD], cos, sin) * factor
        queries[h // GROUP, h % GROUP, :HD, :] = turned.astype(BF16)
        queries[h // GROUP, h % GROUP, HD:, :] = jnp.zeros((HD, raw.shape[1]), BF16)


def values_and_ones(packed):
    ones = jnp.ones((16, packed.shape[1]), BF16)
    return jnp.concatenate([packed[HD:], ones], axis=0)


def first_unit(g, queries, packed, out, top, total):
    rows = queries.shape[-1]
    part = rows // 2
    natural = packed.T
    values = values_and_ones(packed)
    items = [(r, c) for r in range(GROUP) for c in range(2)]

    def scores_of(i):
        r, c = items[i]
        return nn(natural[: (c + 1) * part], queries[g, r, :, c * part : (c + 1) * part])

    scores = scores_of(0)
    done = []
    for i, (r, c) in enumerate(items):
        later = scores_of(i + 1) if i + 1 < len(items) else None
        key_at = lax.broadcasted_iota(jnp.int32, scores.shape, 0)
        query_at = lax.broadcasted_iota(jnp.int32, scores.shape, 1) + c * part
        scores = jnp.where(key_at <= query_at, scores, MASKED)
        high = jnp.max(scores, axis=0, keepdims=True)
        probs = jnp.exp2(scores - high)
        done.append((high, nn(values[:, : (c + 1) * part], probs.astype(BF16))))
        scores = later
    for (r, c), (high, summed) in zip(items, done):
        cols = slice(c * part, (c + 1) * part)
        top[g, r, :, cols] = high
        total[g, r, :, cols] = summed[HD : HD + 1]
        out[g, r, :, cols] = summed[:HD]


def next_unit(g, queries, packed, out, top, total):
    natural = packed.T
    values = values_and_ones(packed)
    before = [(top[g, r], total[g, r], out[g, r]) for r in range(GROUP)]
    scores = [nn(natural, queries[g, r]) for r in range(2)]
    done = []
    for r in range(GROUP):
        if r + 2 < GROUP:
            scores.append(nn(natural, queries[g, r + 2]))
        old, count, acc = before[r]
        high = jnp.maximum(old, jnp.max(scores[r], axis=0, keepdims=True))
        probs = jnp.exp2(scores[r] - high)
        fade = jnp.exp2(old - high)
        summed = nn(values, probs.astype(BF16))
        done.append((high, count * fade + summed[HD : HD + 1], acc * fade + summed[:HD]))
    for r, (high, count, acc) in enumerate(done):
        top[g, r] = high
        total[g, r] = count
        out[g, r] = acc


def finish_forward(out, top, total, mixed_t, lse):
    for h in range(H):
        g, r = h // GROUP, h % GROUP
        scaled = out[g, r] * (1.0 / total[g, r])
        out[g, r] = scaled
        mixed_t[h * HD : (h + 1) * HD, :] = scaled.astype(BF16)
        lse[g, r] = top[g, r] + jnp.log2(total[g, r])


def grad_unit(g, queries, d_out, lse, delta, packed, dq, masked):
    rows = queries.shape[-1]
    natural = packed.T

    def d_head(r, first=0):
        start = pl.multiple_of((g * GROUP + r) * PAIR + first, HD)
        return d_out[pl.ds(start, PAIR - first)]

    before = [dq[g, r] for r in range(GROUP)]

    def products(r):
        return nn(natural, queries[g, r]), nn(natural, d_head(r))

    ahead = products(0)
    done = []
    d_keys, d_vals = None, None
    for r in range(GROUP):
        scores, d_probs = ahead
        if r + 1 < GROUP:
            ahead = products(r + 1)
        probs = jnp.exp2(scores - lse[g, r])
        if masked:
            key_at = lax.broadcasted_iota(jnp.int32, scores.shape, 0)
            query_at = lax.broadcasted_iota(jnp.int32, scores.shape, 1)
            probs = jnp.where(key_at <= query_at, probs, 0.0)
        d_scores = (probs * (d_probs - delta[g, r])).astype(BF16)
        keys_term = nt(queries[g, r, :HD], d_scores)
        vals_term = nt(d_head(r, HD), probs.astype(BF16))
        d_keys = keys_term if d_keys is None else d_keys + keys_term
        d_vals = vals_term if d_vals is None else d_vals + vals_term
        done.append(before[r] + nn(packed[:HD], d_scores))
    for r in range(GROUP):
        dq[g, r] = done[r]
    return d_keys * LN2, d_vals


def log2(n):
    return n.bit_length() - 1


class Cube:
    def __init__(self, s, b, sizes, send_sem, recv_sem, credit):
        seqs, blocks = sizes
        self.send_sem, self.recv_sem, self.credit = send_sem, recv_sem, credit
        self.partners, self.bits = [], []
        for bit in range(log2(seqs)):
            mine = (s // 2**bit) % 2
            self.bits.append(mine)
            self.partners.append((s + 2**bit * (1 - 2 * mine), b))
        for bit in range(log2(blocks)):
            mine = (b // 2**bit) % 2
            self.bits.append(mine)
            self.partners.append((s, b + 2**bit * (1 - 2 * mine)))
        self.depth = len(self.bits)

    def span(self, rows, d):
        lo, size = 0, rows
        for e in range(1, d + 1):
            size = size // 2
            lo = lo + self.bits[e] * size
        return lo, size

    def remote(self, src, dst, sem, d):
        i, k = sem
        return pltpu.make_async_remote_copy(
            src_ref=src,
            dst_ref=dst,
            send_sem=self.send_sem.at[i, k],
            recv_sem=self.recv_sem.at[i, k],
            device_id=self.partners[d],
            device_id_type=MESH,
        )

    def scatter(self, part, landing, i, d):
        mine = self.bits[0]
        if d == 0:
            src = part.at[1 - mine]
        else:
            before, _ = self.span(part.shape[1], d - 1)
            _, size = self.span(part.shape[1], d)
            start = pl.multiple_of(before + (1 - self.bits[d]) * size, 16)
            src = part.at[mine, pl.ds(start, size)]
        return self.remote(src, landing[d], (i, d), d)

    def gather(self, part, i, d):
        lo, size = self.span(part.shape[1], d)
        ref = part.at[self.bits[0], pl.ds(pl.multiple_of(lo, 16), size)]
        return self.remote(ref, ref, (i, self.depth + d), d)

    def add(self, part, landing, d):
        lo, size = self.span(part.shape[1], d)
        rows = pl.ds(pl.multiple_of(lo, 16), size)
        mine = self.bits[0]
        part[mine, rows] = (part[mine, rows].astype(F32) + landing[d][...].astype(F32)).astype(BF16)

    def step(self, part, landing, i, k):
        n = self.depth
        if k < n:
            sent = self.scatter(part, landing, i, k)
            sent.wait_send()
            pl.semaphore_signal(
                self.credit.at[i, k], inc=1, device_id=self.partners[k], device_id_type=MESH
            )
            sent.wait_recv()
            self.add(part, landing, k)
            if k + 1 < n:
                self.scatter(part, landing, i, k + 1).start()
            else:
                self.send_back(part, i, n - 1)
        else:
            d = 2 * n - 1 - k
            self.gather(part, i, d).wait_recv()
            if d > 0:
                self.send_back(part, i, d - 1)

    def send_back(self, part, i, d):
        pl.semaphore_wait(self.credit.at[i, d], 1)
        self.gather(part, i, d).start()

    def drain(self, part, i):
        for d in range(self.depth):
            self.gather(part, i, d).wait_send()


def padded_rows(rows, depth):
    unit = 16 * 2 ** (depth - 1)
    return (rows + unit - 1) // unit * unit


def mega_kernel(
    sizes,
    keep_mask, keep_rate, exit_scales,
    tokens, groups, gain1, gain2, wk, wv, wq, cos, sin,
    wo_hbm, wg_hbm, wu_hbm, wd_hbm, cot_hbm,
    layer_out, input_grad, parts, tail,
    wo, stream, cotangent,
    queries, kv_all, attended, mixed_t, top, total,
    d_normed2, d_out,
    chain, cross,
    load_sem, stream_sem, send_sem, recv_sem, cube_send, cube_recv, credit, kv_send, chain_recv, cross_recv,
    *landings,
):
    seqs, blocks = sizes
    s, b = lax.axis_index("seq"), lax.axis_index("blk")
    z, y, floors = b // 2, b % 2, blocks // 2
    above, below, across = (s, b + 2), (s, b - 2), (s, b + 1 - 2 * y)
    has_above, has_below = z < floors - 1, z > 0
    cube = Cube(s, b, sizes, cube_send, cube_recv, credit)
    depth = cube.depth
    count = parts.shape[0]
    main_landing, tail_landing = landings[:depth], landings[depth:]

    loads = [
        pltpu.make_async_copy(src, dst, load_sem.at[i])
        for i, (src, dst) in enumerate(
            [(wo_hbm, wo), (cot_hbm, cotangent)]
        )
    ]
    step = 2 * LANES
    chunks = wg_hbm.shape[1] // step

    def weights(f):
        at = pl.ds(pl.multiple_of(f * step, step), step)
        return [
            pltpu.make_async_copy(ref.at[:, at], stream.at[f % 2, k], stream_sem.at[f % 2, k])
            for k, ref in enumerate((wg_hbm, wu_hbm, wd_hbm))
        ]

    for load in loads + weights(0):
        load.start()

    barrier = pltpu.get_barrier_semaphore()

    def greet(device):
        pl.semaphore_signal(barrier, inc=1, device_id=device, device_id_type=MESH)

    for device in cube.partners:
        greet(device)
    odd = z % 2
    extra_below = has_below & (odd == 0)
    extra_above = has_above & (odd == 1)

    @pl.when(extra_below)
    def _():
        greet(below)

    @pl.when(extra_above)
    def _():
        greet(above)

    extra = extra_below.astype(jnp.int32) + extra_above.astype(jnp.int32)

    def copy(kind, j, g):
        return pltpu.make_async_remote_copy(
            src_ref=kv_all.at[j, g],
            dst_ref=kv_all.at[j, g],
            send_sem=send_sem.at[kind, j, g],
            recv_sem=recv_sem.at[j, g],
            device_id=above if kind == 0 else across,
            device_id_type=MESH,
        )

    normed = normalize(tokens, gain1)
    c, sn = cos[...], sin[...]
    project_kv(normed, wk, wv, c, sn, kv_all.at[b])
    pl.semaphore_wait(barrier, depth + extra)

    def send_own(g, carry):
        @pl.when(has_above)
        def _():
            copy(0, b, g).start()

        @pl.when(y == 0)
        def _():
            copy(1, b, g).start()

        return carry

    lax.fori_loop(0, KVH, send_own, 0)
    project_q(normed, wq, c, sn, queries)

    def own(g, carry):
        first_unit(g, queries, kv_all[b, g], attended, top, total)
        return carry

    lax.fori_loop(0, KVH, own, 0)

    def level(m, carry):
        def one(g, inner):
            @pl.when(m <= z)
            def _():
                j = b - 2 * m
                copy(0, j, g).wait_recv()

                @pl.when(has_above)
                def _():
                    copy(0, j, g).start()

                copy(1, j, g).start()
                next_unit(g, queries, kv_all[j, g], attended, top, total)

            @pl.when((m >= 2) | (y == 1))
            def _():
                j = b - 2 * m + 3 - 2 * y
                copy(1, j, g).wait_recv()
                next_unit(g, queries, kv_all[j, g], attended, top, total)

            return inner

        return lax.fori_loop(0, KVH, one, carry)

    lax.fori_loop(1, z + 2, level, 0)
    lse = top
    finish_forward(attended, top, total, mixed_t, lse)

    def drain_forward(m, carry):
        def one(g, inner):
            j = b - 2 * m

            @pl.when(has_above)
            def _():
                copy(0, j, g).wait_send()

            @pl.when((m >= 1) | (y == 0))
            def _():
                copy(1, j, g).wait_send()

            return inner

        return lax.fori_loop(0, KVH, one, carry)

    lax.fori_loop(0, z + 1, drain_forward, 0)

    lead = count + 1
    start, stride = [1 - lead], [1]
    for d in range(1, depth):
        start.append(2 * d - 7)
        stride.append(2)
    for d in range(depth - 1, 1, -1):
        start.append(start[-1] + 2)
        stride.append(2)
    start += [start[-1] + 3, start[-1] + 4]
    stride += [2, 2]
    slots = max(KVH * blocks + 2 * floors + 2, start[-1] + 2 * count)
    shift = 2 * lead + 2 * depth

    def serve(n):
        for k in range(2 * depth - 1, -1, -1):
            at = n - start[k] + 2 * shift
            i = at // stride[k] - 2 * shift // stride[k]
            due = (at % stride[k] == 0) & (i >= 0) & (i < count)

            @pl.when(due)
            def _(i=i, k=k):
                cube.step(parts.at[i], [r.at[i] for r in main_landing], i, k)

    for load in loads:
        load.wait()
    bs = keep_mask[0].astype(F32) * keep_rate[0]
    gain = column(gain2[...])
    hidden = tokens[...].astype(F32) + bs * nn(wo[...].T, mixed_t[...])
    r2 = inverse_rms(hidden)
    normed2_t = (hidden * r2 * gain).astype(BF16)
    normed2 = normed2_t.T

    def seed():
        by_group = jnp.where(groups[...] == 1, exit_scales[1], exit_scales[0])
        return cotangent[...].astype(F32) * by_group

    d_down_t = (bs * seed()).astype(BF16)
    d_down = d_down_t.T
    width, rows = hidden.shape
    for i in range(count):
        filled = 3 * width if i < chunks else 5 * width // 2
        for half in range(2):
            parts[i, half, filled:] = jnp.zeros((parts.shape[2] - filled, LANES), BF16)
    down = d_hidden = input_grad
    down[...] = jnp.zeros_like(down)
    d_normed2[...] = jnp.zeros_like(d_normed2)

    def chunk(f, carry):
        for load in weights(f):
            load.wait()

        @pl.when(f + 1 < chunks)
        def _():
            for load in weights(f + 1):
                load.start()

        wg, wu, wd = (stream.at[f % 2, k] for k in range(3))
        gate = nn(normed2, wg[...])
        up = nn(normed2, wu[...])
        d_act = nn(d_down, wd[...])
        sig = 1.0 / (1.0 + jnp.exp(-gate))
        silu = gate * sig
        act = (silu * up).astype(BF16)
        d_gate = (d_act * up * (sig + silu * (1.0 - sig))).astype(BF16)
        d_up = (d_act * silu).astype(BF16)
        grads = (nn(normed2_t, d_gate), nn(normed2_t, d_up), nn(d_down_t, act))
        for k, value in enumerate(grads):
            for half in range(2):
                parts[f, half, k * width : (k + 1) * width] = value[
                    :, half * LANES : (half + 1) * LANES
                ].astype(BF16)
        down[...] += nt(wd[...], act)
        d_normed2[...] += nt(wg[...], d_gate) + nt(wu[...], d_up)
        cube.scatter(parts.at[f], [r.at[f] for r in main_landing], f, 0).start()
        serve(f - lead)
        return carry

    lax.fori_loop(0, chunks, chunk, 0)
    layer_out[...] = (hidden + bs * down[...]).astype(BF16)
    dn = d_normed2[...]
    gain2_grad = jnp.sum(dn * hidden * r2, axis=1, keepdims=True)
    gained = gain * dn
    dh = seed() + r2 * gained - hidden * (r2 * r2 * r2) * jnp.mean(gained * hidden, axis=0, keepdims=True)
    d_hidden[...] = dh
    d_branch = (bs * dh).astype(BF16)
    out_grad = nt(mixed_t[...], d_branch)
    half_rows = width // 2
    last = parts.at[chunks]
    last[0, :width] = out_grad[:, :LANES].astype(BF16)
    last[0, width : 2 * width] = out_grad[:, LANES : 2 * LANES].astype(BF16)
    middle = out_grad[:, 2 * LANES : 3 * LANES].astype(BF16)
    last[0, 2 * width : 2 * width + half_rows] = middle[:half_rows]
    last[1, :half_rows] = middle[half_rows:]
    last[1, half_rows : half_rows + width] = out_grad[:, 3 * LANES : 4 * LANES].astype(BF16)
    last[1, half_rows + width : half_rows + 2 * width] = with_gain(out_grad, gain2_grad)
    cube.scatter(last, [r.at[chunks] for r in main_landing], chunks, 0).start()
    serve(-2)
    d_mixed = nn(wo[...], d_branch).astype(BF16)
    delta = total
    for h in range(H):
        g, r = h // GROUP, h % GROUP
        head = d_mixed[h * HD : (h + 1) * HD]
        d_out[h * PAIR : h * PAIR + HD] = jnp.zeros((HD, rows), BF16)
        d_out[h * PAIR + HD : (h + 1) * PAIR] = head
        delta[g, r] = jnp.sum(head.astype(F32) * attended[g, r], axis=0, keepdims=True)
    dq = attended
    dq[...] = jnp.zeros_like(dq)
    serve(-1)

    def kv_down(j, g):
        return pltpu.make_async_remote_copy(
            src_ref=kv_all.at[j, g],
            dst_ref=chain.at[j // 2, g],
            send_sem=kv_send.at[j, g],
            recv_sem=chain_recv.at[j // 2, g],
            device_id=below,
            device_id_type=MESH,
        )

    def kv_across(j, g):
        return pltpu.make_async_remote_copy(
            src_ref=kv_all.at[j, g],
            dst_ref=cross.at[j // 2, g],
            send_sem=kv_send.at[j, g],
            recv_sem=cross_recv.at[j // 2, g],
            device_id=across,
            device_id_type=MESH,
        )

    d_kv = d_normed2
    lag = 2 + 2 * (floors - 1 - z)

    def slot(n, carry):
        j, g = n // KVH, n % KVH

        def unit(masked):
            d_keys, d_vals = grad_unit(g, queries, d_out, lse, delta, kv_all[j, g], dq, masked)
            kv_all[j, g, :HD] = d_keys.astype(BF16)
            kv_all[j, g, HD:] = d_vals.astype(BF16)

        @pl.when(j < b)
        def _():
            unit(False)

        @pl.when(j == b)
        def _():
            unit(True)

        @pl.when((j <= b) & (j % 2 != y))
        def _():
            kv_across(j, g).start()

        ready = n - lag + KVH * blocks
        jj, gg = ready // KVH - blocks, ready % KVH

        @pl.when((n >= lag) & (jj <= b) & (jj % 2 == y))
        def _():
            at = pl.ds(pl.multiple_of(gg * PAIR, PAIR), PAIR)
            mine = kv_all[jj, gg].astype(F32)
            d_kv[at] = mine

            @pl.when((jj < b) | (y == 0))
            def _():
                kv_across(jj, gg).wait_recv()
                d_kv[at] = d_kv[at] + cross[jj // 2, gg].astype(F32)

            @pl.when(has_above)
            def _():
                kv_down(jj, gg).wait_recv()
                d_kv[at] = d_kv[at] + chain[jj // 2, gg].astype(F32)

            @pl.when(jj < b)
            def _():
                kv_all[jj, gg] = d_kv[at].astype(BF16)
                kv_down(jj, gg).start()

        serve(n)
        return carry

    lax.fori_loop(0, slots, slot, 0)

    def drain_backward(n, carry):
        j, g = n // KVH, n % KVH

        @pl.when(j % 2 != y)
        def _():
            kv_across(j, g).wait_send()

        @pl.when((j % 2 == y) & (j < b))
        def _():
            kv_down(j, g).wait_send()

        return carry

    lax.fori_loop(0, KVH * (b + 1), drain_backward, 0)

    x = tokens[...].astype(F32)
    r1 = inverse_rms(x)
    weight = column(gain1[...])
    normed = (x * r1 * weight).astype(BF16)
    c, sn = cos[...], -sin[...]
    nq, nk = H * HD, KVH * HD
    turned = d_out
    for h in range(H):
        piece = dq[h // GROUP, h % GROUP] * HD**-0.5
        turned[h * HD : (h + 1) * HD, :] = turn(piece, c, sn).astype(BF16)
    for g in range(KVH):
        turned[nq + g * HD : nq + (g + 1) * HD, :] = turn(d_kv[g * PAIR : g * PAIR + HD], c, sn).astype(BF16)
        turned[nq + nk + g * HD : nq + nk + (g + 1) * HD, :] = d_kv[g * PAIR + HD : (g + 1) * PAIR].astype(BF16)
    d_normed = (
        nn(wq[...], turned[:nq, :])
        + nn(wk[...].T, turned[nq : nq + nk, :])
        + nn(wv[...].T, turned[nq + nk : nq + 2 * nk, :])
    )
    query_grad = nt(normed, turned[:nq, :])
    kv_grad = nt(turned[nq : nq + 2 * nk, :], normed)
    gain1_grad = jnp.sum(d_normed * x * r1, axis=1, keepdims=True)
    for i in range(4):
        tail[0, i * width : (i + 1) * width] = query_grad[:, i * LANES : (i + 1) * LANES].astype(BF16)
    tail[0, 4 * width :] = jnp.zeros((tail.shape[1] - 4 * width, LANES), BF16)
    tail[1, :width] = with_gain(query_grad, gain1_grad)
    for i in range(5):
        first = width + i * 2 * nk
        left = kv_grad[:, i * LANES : (i + 1) * LANES].astype(BF16)
        if left.shape[1] < LANES:
            left = jnp.concatenate([left, jnp.zeros_like(left)], axis=1)
        tail[1, first : first + 2 * nk] = left
    filled = width + 10 * nk
    tail[1, filled:] = jnp.zeros((tail.shape[1] - filled, LANES), BF16)
    cube.scatter(tail, tail_landing, count, 0).start()
    gained = weight * d_normed
    input_grad[...] = (
        d_hidden[...] + r1 * gained - x * (r1 * r1 * r1) * jnp.mean(gained * x, axis=0, keepdims=True)
    )
    for k in range(2 * depth):
        cube.step(tail, tail_landing, count, k)
    for i in range(count):
        cube.drain(parts.at[i], i)
    cube.drain(tail, count)


def unpack_kernel(
    chunks, parts, tail, gate, up, down, output, query, key, value, gain1, gain2
):
    i = pl.program_id(0)
    width = gate.shape[0]

    @pl.when(i < chunks)
    def _():
        for k, out in enumerate((gate, up, down)):
            for half in range(2):
                piece = parts[0, half, k * width : (k + 1) * width]
                out[:, half * LANES : (half + 1) * LANES] = piece.astype(F32)

    @pl.when(i == chunks)
    def _():
        half = width // 2
        output[:, :LANES] = parts[0, 0, :width].astype(F32)
        output[:, LANES : 2 * LANES] = parts[0, 0, width : 2 * width].astype(F32)
        output[:half, 2 * LANES : 3 * LANES] = parts[0, 0, 2 * width : 2 * width + half].astype(F32)
        output[half:, 2 * LANES : 3 * LANES] = parts[0, 1, :half].astype(F32)
        output[:, 3 * LANES : 4 * LANES] = parts[0, 1, half : half + width].astype(F32)
        end = parts[0, 1, half + width : half + 2 * width].astype(F32)
        output[:, 4 * LANES :] = end[:, :HD]
        gain2[...] = end.T[HD : HD + 1]
        for k in range(4):
            query[:, k * LANES : (k + 1) * LANES] = tail[0, k * width : (k + 1) * width].astype(F32)
        end = tail[1, :width].astype(F32)
        query[:, 4 * LANES :] = end[:, :HD]
        gain1[...] = end.T[HD : HD + 1]
        nk = key.shape[0]
        for k in range(5):
            size = min(LANES, width - k * LANES)
            lanes = slice(k * LANES, k * LANES + size)
            first = width + 2 * k * nk
            key[:, lanes] = tail[1, first : first + nk].astype(F32)[:, :size]
            value[:, lanes] = tail[1, first + nk : first + 2 * nk].astype(F32)[:, :size]


def with_gain(grad, gain):
    rows = grad.shape[0]
    return jnp.concatenate(
        [grad[:, 4 * LANES :], gain, jnp.zeros((rows, LANES - HD - 1), F32)], axis=1
    ).astype(BF16)


def body(sizes, tokens, positions, groups, keep_mask, exit_scales, keep_rate, wq, wk, wv, wo, wg, wu, wd, gain1, gain2, cotangent):
    seqs, blocks = sizes
    depth = log2(seqs) + log2(blocks)
    tokens, cotangent = tokens[0].T, cotangent[0].T
    wk, wv, wd = wk.T, wv.T, wd.T
    width, rows = tokens.shape
    ff = wg.shape[1]
    nq, nk = H * HD, KVH * HD
    frequency = 1.0 / ROPE_BASE ** (jnp.arange(HALF, dtype=F32) * (2.0 / HD))
    angle = frequency[:, None] * positions[0].astype(F32)[None, :]
    cos, sin = jnp.cos(angle), jnp.sin(angle)

    chunks = ff // (2 * LANES)
    count = chunks + 1
    part_rows = padded_rows(3 * width, depth)
    tail_rows = padded_rows(max(4 * width, width + 10 * nk), depth)
    vmem, smem, hbm = (pl.BlockSpec(memory_space=m) for m in (pltpu.VMEM, pltpu.SMEM, pl.ANY))
    head_t = (KVH, GROUP, PAIR, rows)
    head_o = (KVH, GROUP, HD, rows)
    head_1 = (KVH, GROUP, 1, rows)
    dma = pltpu.SemaphoreType.DMA
    scratch = [
        pltpu.VMEM(wo.shape, BF16),
        pltpu.VMEM((2, 3, width, 2 * LANES), BF16),
        pltpu.VMEM(cotangent.shape, BF16),
        pltpu.VMEM(head_t, BF16),
        pltpu.VMEM((blocks, KVH, PAIR, rows), BF16),
        pltpu.VMEM(head_o, F32),
        pltpu.VMEM((nq, rows), BF16),
        pltpu.VMEM(head_1, F32),
        pltpu.VMEM(head_1, F32),
        pltpu.VMEM((width, rows), F32),
        pltpu.VMEM((H * PAIR, rows), BF16),
        pltpu.VMEM((blocks // 2, KVH, PAIR, rows), BF16),
        pltpu.VMEM((blocks // 2, KVH, PAIR, rows), BF16),
        dma((2,)),
        dma((2, 3)),
        dma((2, blocks, KVH)),
        dma((blocks, KVH)),
        dma((count + 1, 2 * depth)),
        dma((count + 1, 2 * depth)),
        pltpu.SemaphoreType.REGULAR((count + 1, depth)),
        dma((blocks, KVH)),
        dma((blocks // 2, KVH)),
        dma((blocks // 2, KVH)),
    ]
    scratch += [pltpu.VMEM((count, part_rows >> d, LANES), BF16) for d in range(depth)]
    scratch += [pltpu.VMEM((tail_rows >> d, LANES), BF16) for d in range(depth)]
    layer_out, input_grad, parts, tail = pl.pallas_call(
        functools.partial(mega_kernel, sizes),
        out_shape=[
            jax.ShapeDtypeStruct((width, rows), BF16),
            jax.ShapeDtypeStruct((width, rows), F32),
            jax.ShapeDtypeStruct((count, 2, part_rows, LANES), BF16),
            jax.ShapeDtypeStruct((2, tail_rows, LANES), BF16),
        ],
        in_specs=[smem] * 3 + [vmem] * 9 + [hbm] * 5,
        out_specs=[vmem] * 4,
        scratch_shapes=scratch,
        compiler_params=pltpu.CompilerParams(
            vmem_limit_bytes=VMEM_LIMIT, collective_id=0, has_side_effects=True
        ),
    )(
        keep_mask, keep_rate, exit_scales,
        tokens, groups, gain1[None, :], gain2[None, :], wk, wv, wq, cos, sin,
        wo, wg, wu, wd, cotangent,
    )

    wide = pl.BlockSpec((width, 2 * LANES), lambda i: (0, jnp.minimum(i, chunks - 1)))
    small = [(nq, width), (width, nq), (nk, width), (nk, width), (1, width), (1, width)]
    gate_grad, up_grad, down_grad, output_grad, query_grad, key_grad, value_grad, gain1_grad, gain2_grad = pl.pallas_call(
        functools.partial(unpack_kernel, chunks),
        grid=(count,),
        out_shape=[jax.ShapeDtypeStruct((width, ff), F32)] * 3
        + [jax.ShapeDtypeStruct(shape, F32) for shape in small],
        in_specs=[
            pl.BlockSpec((1, 2, part_rows, LANES), lambda i: (i, 0, 0, 0)),
            pl.BlockSpec(tail.shape, lambda i: (0, 0, 0)),
        ],
        out_specs=[wide] * 3 + [pl.BlockSpec(shape, lambda i: (0, 0)) for shape in small],
        compiler_params=pltpu.CompilerParams(vmem_limit_bytes=VMEM_LIMIT),
    )(parts, tail)
    return (
        layer_out.T[None],
        input_grad.T[None],
        query_grad,
        key_grad.T,
        value_grad.T,
        output_grad,
        gate_grad,
        up_grad,
        down_grad.T,
        gain1_grad[0],
        gain2_grad[0],
    )


def solution(mesh):
    local = P("seq", "blk", None)
    pair = P("seq", "blk")
    placed = (local, pair, pair, P("seq")) + (P(),) * 11 + (local,)
    return jax.shard_map(
        functools.partial(body, (mesh.shape["seq"], mesh.shape["blk"])),
        mesh=mesh,
        in_specs=placed,
        out_specs=(local, local) + (P(),) * 9,
        check_vma=False,
    )
```

time: 410 us -> 214 us (0.52)
  waiting for transfers between devices: 276 us -> 0 us
  Pallas kernels: 52.4 us -> 201 us
  blocking collectives: 41.6 us -> 0 us
  other arithmetic: 19 us -> 4.33 us
  between operations: 15.4 us -> 1.97 us
    reduce_scatter x1 -> x0, waiting for transfers between devices: 149 us -> none  [body(): lax.psum_scatter(d_kv, 'blk', scatter_dimension=0, tiled=False).astype(F32)]
    pallas_call x4 -> x2, Pallas kernels: 52.4 us -> 201 us  [the longest x1 190 us: body(): pl.pallas_call(functools.partial(mega_kernel, sizes), out_shape=[jax.Shap...]
    psum x1 -> x0, waiting for transfers between devices: 127 us -> none  [body(): late = lax.psum((query_grad, key_grad, value_grad), ('seq', 'blk'))]
    psum x1 -> x0, blocking collectives: 41.6 us -> none  [body(): lax.psum(jnp.concatenate([gain1_grad, gain2_grad], axis=1), ('seq', 'blk'))]
    convert_element_type x5 -> x0, other arithmetic: 8.92 us -> none  [the longest x1 2.26 us: body(): early[1].astype(F32)]
    transpose x3 -> x0, other arithmetic: 5.89 us -> none  [the longest x1 2.26 us: body(): early[2].astype(F32)]
  transfers between devices with their start and end apart: 2 -> 0, of which waited for: 2 -> 0; matrix products, arithmetic and copies ran while one was open for 0% -> 0% of each run, Pallas kernels for 0% -> 0%
where the time goes in v3:
time: 214 us; the launch traced here: 212 us
  Pallas kernels  201 us (94%)
  local copies, waits for them, and re-layouts  4.37 us (2%)
  other arithmetic  4.33 us (2%)
    pallas_call x1, Pallas kernels, body(): pl.pallas_call(functools.partial(mega_kernel, sizes), out_shape=[jax.Shap...  190 us
    pallas_call x1, Pallas kernels, body(): pl.pallas_call(functools.partial(unpack_kernel, chunks), grid=(count,), o...  10.7 us

profile of v3, /device:TPU:0, one launch (start us, length us, event | category | flops | bytes accessed | tf_op | source)
XLA Modules:
  0.0 211.8 jit_solution(15660275240806791654)
XLA Ops:
  1.9 0.7 convert_element_type.4
  2.6 1.3 broadcast_in_dim.14.gain1
  3.9 1.3 broadcast_in_dim.15.gain2
  5.2 1.0 multiply_sine_fusion
  6.1 190.5 %shard_map.239 = (bf16[576,512]{1,0:T(8,128)(2,1)}, f32[576,512]{1,0:T(8,128)}, bf16[7,2,1792,128]{3,2,1,0:T(8,128)(2,1)}, bf16[2,2560,128]{2,1,0:T(8,128)(2,1)}) custom-call(s32[1]{0:T(128)S(6)} %copy.29.keep_mask, f32[1]{0:T(128)S(6)} %copy.30.keep_rate, f32[2]{0:T(128)} %exit_scales.1, bf16[576,512]{1,0:T(8,128)(2,1)} %bitcast.21, s32[1,512]{1,0:T(1,128)} %groups.1, ...), custom_call_target="tpu_custom_call" | custom-call | tf_op jit(solution)/shard_map/pallas_call | solution.py:744
  196.6 0.0 copy-start.1
  196.6 10.7 %shard_map.240 = (f32[576,1536]{1,0:T(8,128)}, f32[576,1536]{1,0:T(8,128)}, f32[576,1536]{1,0:T(8,128)}, f32[576,576]{1,0:T(8,128)}, f32[576,576]{1,0:T(8,128)},...) custom-call(bf16[7,2,1792,128]{3,2,1,0:T(8,128)(2,1)} %get-tuple-element.26.parts, ...), custom_call_target="tpu_custom_call" | custom-call | tf_op jit(solution)/shard_map/pallas_call | solution.py:766
  207.3 0.0 copy-start
  207.3 1.4 reduce
  208.7 1.3 reduce.1
  210.0 0.0 copy-done.1
  210.0 0.8 copy.31
  210.8 0.0 copy-done
  210.8 1.0 copy.32
  (1 shorter events, 0.0 us)
Async XLA Ops:
  196.6 13.4 %copy-start.1 = (bf16[576,512]{1,0:T(8,128)(2,1)S(1)}, bf16[576,512]{1,0:T(8,128)(2,1)}, u32[]{:S(2)}) copy-start(bf16[576,512]{1,0:T(8,128)(2,1)} %get-tuple-element.24) | copy-start | bytes 1769476
  207.3 3.5 %copy-start = (f32[576,512]{1,0:T(8,128)S(1)}, f32[576,512]{1,0:T(8,128)}, u32[]{:S(2)}) copy-start(f32[576,512]{1,0:T(8,128)} %get-tuple-element.25) | copy-start | bytes 3538948

commit v4 on v3

--- a/solution.py
+++ b/solution.py
@@ -34,8 +34,12 @@
     return lax.dot_general(a, b, (((1,), (1,)), ((), ())), preferred_element_type=F32)
 
 
-def column(row):
-    return jnp.broadcast_to(row, (8, row.shape[1])).T[:, :1]
+def column(values):
+    return jnp.broadcast_to(values[None, :], (8, values.shape[0])).T[:, :1]
+
+
+def as_row(values):
+    return jnp.broadcast_to(values, (values.shape[0], 8)).T[:1]
 
 
 def inverse_rms(values):
@@ -174,20 +178,16 @@
     return n.bit_length() - 1
 
 
+HALVINGS = 3
+
+
 class Cube:
-    def __init__(self, s, b, sizes, send_sem, recv_sem, credit):
-        seqs, blocks = sizes
+    def __init__(self, links, send_sem, recv_sem, credit):
         self.send_sem, self.recv_sem, self.credit = send_sem, recv_sem, credit
-        self.partners, self.bits = [], []
-        for bit in range(log2(seqs)):
-            mine = (s // 2**bit) % 2
-            self.bits.append(mine)
-            self.partners.append((s + 2**bit * (1 - 2 * mine), b))
-        for bit in range(log2(blocks)):
-            mine = (b // 2**bit) % 2
-            self.bits.append(mine)
-            self.partners.append((s, b + 2**bit * (1 - 2 * mine)))
-        self.depth = len(self.bits)
+        self.bits = [bit for bit, _ in links]
+        self.partners = [partner for _, partner in links]
+        self.depth = len(links)
+        self.steps = self.depth + HALVINGS
 
     def span(self, rows, d):
         lo, size = 0, rows
@@ -196,8 +196,24 @@
             lo = lo + self.bits[e] * size
         return lo, size
 
-    def remote(self, src, dst, sem, d):
-        i, k = sem
+    def owned(self, part, d):
+        lo, size = self.span(part.shape[1], d)
+        return part.at[self.bits[0], pl.ds(pl.multiple_of(lo, 16), size)]
+
+    def transfer(self, part, landing, i, k):
+        mine, d = self.bits[0], k
+        if k == 0:
+            src, dst = part.at[1 - mine], landing[0]
+        elif k < HALVINGS:
+            before, _ = self.span(part.shape[1], k - 1)
+            _, size = self.span(part.shape[1], k)
+            start = pl.multiple_of(before + (1 - self.bits[k]) * size, 16)
+            src, dst = part.at[mine, pl.ds(start, size)], landing[k]
+        elif k < self.depth:
+            src, dst = self.owned(part, HALVINGS - 1), landing[k]
+        else:
+            d = self.steps - 1 - k
+            src = dst = self.owned(part, d)
         return pltpu.make_async_remote_copy(
             src_ref=src,
             dst_ref=dst,
@@ -207,60 +223,97 @@
             device_id_type=MESH,
         )
 
-    def scatter(self, part, landing, i, d):
-        mine = self.bits[0]
-        if d == 0:
-            src = part.at[1 - mine]
-        else:
-            before, _ = self.span(part.shape[1], d - 1)
-            _, size = self.span(part.shape[1], d)
-            start = pl.multiple_of(before + (1 - self.bits[d]) * size, 16)
-            src = part.at[mine, pl.ds(start, size)]
-        return self.remote(src, landing[d], (i, d), d)
-
-    def gather(self, part, i, d):
-        lo, size = self.span(part.shape[1], d)
-        ref = part.at[self.bits[0], pl.ds(pl.multiple_of(lo, 16), size)]
-        return self.remote(ref, ref, (i, self.depth + d), d)
-
-    def add(self, part, landing, d):
-        lo, size = self.span(part.shape[1], d)
-        rows = pl.ds(pl.multiple_of(lo, 16), size)
-        mine = self.bits[0]
-        part[mine, rows] = (part[mine, rows].astype(F32) + landing[d][...].astype(F32)).astype(BF16)
+    def begin(self, part, landing, i, k):
+        if k >= self.depth:
+            pl.semaphore_wait(self.credit.at[i, self.steps - 1 - k], 1)
+        self.transfer(part, landing, i, k).start()
 
     def step(self, part, landing, i, k):
-        n = self.depth
-        if k < n:
-            sent = self.scatter(part, landing, i, k)
-            sent.wait_send()
-            pl.semaphore_signal(
-                self.credit.at[i, k], inc=1, device_id=self.partners[k], device_id_type=MESH
-            )
-            sent.wait_recv()
-            self.add(part, landing, k)
-            if k + 1 < n:
-                self.scatter(part, landing, i, k + 1).start()
+        moved = self.transfer(part, landing, i, k)
+        if k < self.depth:
+            moved.wait_send()
+            if k < HALVINGS:
+                pl.semaphore_signal(
+                    self.credit.at[i, k], inc=1, device_id=self.partners[k], device_id_type=MESH
+                )
+        moved.wait_recv()
+        if k < self.depth:
+            rows = self.owned(part, min(k, HALVINGS - 1))
+            rows[...] = rows[...] + landing[k][...]
+        if k + 1 < self.steps:
+            self.begin(part, landing, i, k + 1)
+
+    def drain(self, part, landing, i):
+        for k in range(self.depth, self.steps):
+            self.transfer(part, landing, i, k).wait_send()
+
+
+MAIN_SLOTS = [
+    [-7, -5, -3, -1, 1, 4, 6, 8],
+    [-6, -4, -2, 0, 2, 5, 10, 12],
+    [-5, -2, 0, 2, 5, 7, 9, 11],
+    [-4, -1, 1, 3, 9, 11, 16, 20],
+    [-3, 0, 2, 4, 8, 10, 13, 23],
+    [1, 3, 7, 9, 13, 14, 17, 23],
+    [-1, 6, 8, 11, 14, 16, 20, 22],
+]
+LATE_SLOTS = [[13, 14, 16, 17, 18, 19, 22, 23], [18, 19, 20, 21, 22, 23, 25, 28]]
+LAGS = [7, 6, 3, 2]
+
+
+def tables(count, depth, blocks):
+    if (count, depth, blocks) == (len(MAIN_SLOTS), 5, 8):
+        return MAIN_SLOTS, LATE_SLOTS, LAGS
+    floors = blocks // 2
+    main = []
+    for i in range(count):
+        row = [i - count, 2 * i - count + 2]
+        row += [2 * (i + k) - count for k in range(HALVINGS - 1, depth + 1)]
+        main.append(row + [row[-1] + 3 + i // 2, row[-1] + 4 + i // 2])
+    waits = [1, 3, 4] + list(range(5, 2 * depth - 1, 2))
+    waits += [waits[-1] + 1, waits[-1] + 3, waits[-1] + 4]
+    late = [[g * blocks + blocks + 1 + w for w in waits] for g in range(KVH - 1)]
+    return main, late, [2 * (floors - z) for z in range(floors)]
+
+
+def rounds(slots, first, last):
+    lists = []
+    for i, n in enumerate(slots):
+        if first <= n < last:
+            for chosen in lists:
+                if all(n != other for _, other in chosen):
+                    chosen.append((i, n))
+                    break
             else:
-                self.send_back(part, i, n - 1)
-        else:
-            d = 2 * n - 1 - k
-            self.gather(part, i, d).wait_recv()
-            if d > 0:
-                self.send_back(part, i, d - 1)
-
-    def send_back(self, part, i, d):
-        pl.semaphore_wait(self.credit.at[i, d], 1)
-        self.gather(part, i, d).start()
-
-    def drain(self, part, i):
-        for d in range(self.depth):
-            self.gather(part, i, d).wait_send()
-
-
-def padded_rows(rows, depth):
-    unit = 16 * 2 ** (depth - 1)
-    return (rows + unit - 1) // unit * unit
+                lists.append([(i, n)])
+    return lists
+
+
+def at_slot(chosen, n):
+    found = 0
+    for i, slot in chosen:
+        found = found + jnp.where(n == slot, i + 1, 0)
+    return found
+
+
+def cube_links(s, b, sizes):
+    seqs, blocks = sizes
+    links = []
+    for bit in range(log2(seqs)):
+        mine = (s // 2**bit) % 2
+        links.append((mine, (s + 2**bit * (1 - 2 * mine), b)))
+    for bit in range(log2(blocks)):
+        mine = (b // 2**bit) % 2
+        links.append((mine, (s, b + 2**bit * (1 - 2 * mine))))
+    return links
+
+
+def row_counts(rows, depth):
+    return [rows >> min(k, HALVINGS - 1) for k in range(depth)]
+
+
+def padded_rows(rows):
+    return (rows + 63) // 64 * 64
 
 
 def mega_kernel(
@@ -268,12 +321,13 @@
     keep_mask, keep_rate, exit_scales,
     tokens, groups, gain1, gain2, wk, wv, wq, cos, sin,
     wo_hbm, wg_hbm, wu_hbm, wd_hbm, cot_hbm,
-    layer_out, input_grad, parts, tail,
+    layer_out, input_grad, parts, tails, gains,
     wo, stream, cotangent,
     queries, kv_all, attended, mixed_t, top, total,
     d_normed2, d_out,
     chain, cross,
-    load_sem, stream_sem, send_sem, recv_sem, cube_send, cube_recv, credit, kv_send, chain_recv, cross_recv,
+    load_sem, stream_sem, send_sem, recv_sem, cube_send, cube_recv, credit, tail_send, tail_recv, tail_credit,
+    gain_send, gain_recv, kv_send, chain_recv, cross_recv, gain_landing,
     *landings,
 ):
     seqs, blocks = sizes
@@ -281,10 +335,17 @@
     z, y, floors = b // 2, b % 2, blocks // 2
     above, below, across = (s, b + 2), (s, b - 2), (s, b + 1 - 2 * y)
     has_above, has_below = z < floors - 1, z > 0
-    cube = Cube(s, b, sizes, cube_send, cube_recv, credit)
+    links = cube_links(s, b, sizes)
+    cube = Cube(links, cube_send, cube_recv, credit)
+    tail_cube = Cube(links, tail_send, tail_recv, tail_credit)
     depth = cube.depth
     count = parts.shape[0]
-    main_landing, tail_landing = landings[:depth], landings[depth:]
+
+    def main(i):
+        return parts.at[i], [r.at[i] for r in landings[:depth]], i
+
+    def late(i):
+        return tails.at[i], [r.at[i] for r in landings[depth:]], i
 
     loads = [
         pltpu.make_async_copy(src, dst, load_sem.at[i])
@@ -407,28 +468,33 @@
 
     lax.fori_loop(0, z + 1, drain_forward, 0)
 
+    whole_head = 2 * floors + 1
+    end = (KVH - 1) * blocks + whole_head + 2
+    main_slots, late_slots, lags = tables(count, depth, blocks)
     lead = count + 1
-    start, stride = [1 - lead], [1]
-    for d in range(1, depth):
-        start.append(2 * d - 7)
-        stride.append(2)
-    for d in range(depth - 1, 1, -1):
-        start.append(start[-1] + 2)
-        stride.append(2)
-    start += [start[-1] + 3, start[-1] + 4]
-    stride += [2, 2]
-    slots = max(KVH * blocks + 2 * floors + 2, start[-1] + 2 * count)
-    shift = 2 * lead + 2 * depth
-
-    def serve(n):
-        for k in range(2 * depth - 1, -1, -1):
-            at = n - start[k] + 2 * shift
-            i = at // stride[k] - 2 * shift // stride[k]
-            due = (at % stride[k] == 0) & (i >= 0) & (i < count)
-
-            @pl.when(due)
-            def _(i=i, k=k):
-                cube.step(parts.at[i], [r.at[i] for r in main_landing], i, k)
+
+    def serve(n, first, last):
+        for k in range(cube.steps - 1, -1, -1):
+            for exchange, block_of, slots in (
+                (tail_cube, late, late_slots),
+                (cube, main, main_slots),
+            ):
+                for chosen in rounds([row[k] for row in slots], first, last):
+                    found = at_slot(chosen, n)
+
+                    @pl.when(found > 0)
+                    def _(exchange=exchange, block_of=block_of, k=k, found=found):
+                        exchange.step(*block_of(jnp.maximum(found - 1, 0)), k)
+
+    def serve_now(n):
+        for k in range(cube.steps - 1, -1, -1):
+            for exchange, block_of, slots in (
+                (tail_cube, late, late_slots),
+                (cube, main, main_slots),
+            ):
+                for i, row in enumerate(slots):
+                    if row[k] == n or (n == end + cube.steps - 3 and row[k] > n):
+                        exchange.step(*block_of(i), k)
 
     for load in loads:
         load.wait()
@@ -448,7 +514,7 @@
     width, rows = hidden.shape
     for i in range(count):
         filled = 3 * width if i < chunks else 5 * width // 2
-        for half in range(2):
+        for half in range(2 if filled < parts.shape[2] else 0):
             parts[i, half, filled:] = jnp.zeros((parts.shape[2] - filled, LANES), BF16)
     down = d_hidden = input_grad
     down[...] = jnp.zeros_like(down)
@@ -480,8 +546,8 @@
                 ].astype(BF16)
         down[...] += nt(wd[...], act)
         d_normed2[...] += nt(wg[...], d_gate) + nt(wu[...], d_up)
-        cube.scatter(parts.at[f], [r.at[f] for r in main_landing], f, 0).start()
-        serve(f - lead)
+        cube.begin(*main(f), 0)
+        serve(f - lead, -lead, -2)
         return carry
 
     lax.fori_loop(0, chunks, chunk, 0)
@@ -501,9 +567,9 @@
     last[0, 2 * width : 2 * width + half_rows] = middle[:half_rows]
     last[1, :half_rows] = middle[half_rows:]
     last[1, half_rows : half_rows + width] = out_grad[:, 3 * LANES : 4 * LANES].astype(BF16)
-    last[1, half_rows + width : half_rows + 2 * width] = with_gain(out_grad, gain2_grad)
-    cube.scatter(last, [r.at[chunks] for r in main_landing], chunks, 0).start()
-    serve(-2)
+    last[1, half_rows + width : half_rows + 2 * width] = last_block(out_grad)
+    cube.begin(*main(chunks), 0)
+    serve_now(-2)
     d_mixed = nn(wo[...], d_branch).astype(BF16)
     delta = total
     for h in range(H):
@@ -514,7 +580,9 @@
         delta[g, r] = jnp.sum(head.astype(F32) * attended[g, r], axis=0, keepdims=True)
     dq = attended
     dq[...] = jnp.zeros_like(dq)
-    serve(-1)
+    normed_kept = mixed_t
+    normed_kept[...] = normalize(tokens, gain1)
+    serve_now(-1)
 
     def kv_down(j, g):
         return pltpu.make_async_remote_copy(
@@ -537,56 +605,108 @@
         )
 
     d_kv = d_normed2
-    lag = 2 + 2 * (floors - 1 - z)
+    lag = lags[0]
+    for i in range(1, floors):
+        lag = jnp.where(z == i, lags[i], lag)
+    nq, nk = H * HD, KVH * HD
+    span = GROUP * PAIR
+
+    def finish_head(g):
+        at = pl.multiple_of(g * span, PAIR)
+        c, sn = cos[...], -sin[...]
+        for r in range(GROUP):
+            piece = turn(dq[g, r] * HD**-0.5, c, sn)
+            d_out[pl.ds(at + r * HD, HD)] = piece.astype(BF16)
+        pair = d_kv[pl.ds(pl.multiple_of(g * PAIR, PAIR), PAIR)]
+        d_out[pl.ds(at + GROUP * HD, HD)] = turn(pair[:HD], c, sn).astype(BF16)
+        d_out[pl.ds(at + (GROUP + 1) * HD, HD)] = pair[HD:].astype(BF16)
+        high = (GROUP + 2) * HD
+        grad = nt(d_out[pl.ds(at, high)], normed_kept[...]).astype(BF16)
+        tails[g, 0, :high] = grad[:, :LANES]
+        tails[g, 0, high : 2 * high] = grad[:, LANES : 2 * LANES]
+        tails[g, 0, 2 * high : 5 * high // 2] = grad[: high // 2, 2 * LANES : 3 * LANES]
+        tails[g, 1, : high // 2] = grad[high // 2 :, 2 * LANES : 3 * LANES]
+        tails[g, 1, high // 2 : 3 * high // 2] = grad[:, 3 * LANES : 4 * LANES]
+        tails[g, 1, 3 * high // 2 : 5 * high // 2] = jnp.concatenate(
+            [grad[:, 4 * LANES :], jnp.zeros((high, HD), BF16)], axis=1
+        )
+        for half in range(2):
+            rest = tails.shape[2] - 5 * high // 2
+            tails[g, half, 5 * high // 2 :] = jnp.zeros((rest, LANES), BF16)
+        tail_cube.begin(*late(g), 0)
 
     def slot(n, carry):
-        j, g = n // KVH, n % KVH
+        g, j = n // blocks, n % blocks
+        busy = n < KVH * blocks
 
         def unit(masked):
             d_keys, d_vals = grad_unit(g, queries, d_out, lse, delta, kv_all[j, g], dq, masked)
             kv_all[j, g, :HD] = d_keys.astype(BF16)
             kv_all[j, g, HD:] = d_vals.astype(BF16)
 
-        @pl.when(j < b)
+        @pl.when(busy & (j < b))
         def _():
             unit(False)
 
-        @pl.when(j == b)
+        @pl.when(busy & (j == b))
         def _():
             unit(True)
 
-        @pl.when((j <= b) & (j % 2 != y))
+        @pl.when(busy & (j <= b) & (j % 2 != y))
         def _():
             kv_across(j, g).start()
 
-        ready = n - lag + KVH * blocks
-        jj, gg = ready // KVH - blocks, ready % KVH
-
-        @pl.when((n >= lag) & (jj <= b) & (jj % 2 == y))
-        def _():
-            at = pl.ds(pl.multiple_of(gg * PAIR, PAIR), PAIR)
-            mine = kv_all[jj, gg].astype(F32)
-            d_kv[at] = mine
-
-            @pl.when((jj < b) | (y == 0))
-            def _():
-                kv_across(jj, gg).wait_recv()
-                d_kv[at] = d_kv[at] + cross[jj // 2, gg].astype(F32)
+        ready = n - lag
+        at = jnp.maximum(ready, 0)
+        gg, jj = at // blocks, at % blocks
+        due = (ready >= 0) & (ready < KVH * blocks) & (jj % 2 == y)
+        rows_of = pl.ds(pl.multiple_of(jnp.minimum(gg, KVH - 1) * PAIR, PAIR), PAIR)
+
+        @pl.when(due & (jj < b))
+        def _():
+            kv_across(jj, gg).wait_recv()
+            both = kv_all[jj, gg].astype(F32) + cross[jj // 2, gg].astype(F32)
 
             @pl.when(has_above)
             def _():
                 kv_down(jj, gg).wait_recv()
-                d_kv[at] = d_kv[at] + chain[jj // 2, gg].astype(F32)
-
-            @pl.when(jj < b)
+                kv_all[jj, gg] = (both + chain[jj // 2, gg].astype(F32)).astype(BF16)
+
+            @pl.when(jnp.logical_not(has_above))
             def _():
-                kv_all[jj, gg] = d_kv[at].astype(BF16)
-                kv_down(jj, gg).start()
-
-        serve(n)
+                kv_all[jj, gg] = both.astype(BF16)
+
+            kv_down(jj, gg).start()
+
+        @pl.when(due & (jj == b))
+        def _():
+            d_kv[rows_of] = kv_all[jj, gg].astype(F32)
+
+            @pl.when(y == 0)
+            def _():
+                kv_across(jj, gg).wait_recv()
+                d_kv[rows_of] = d_kv[rows_of] + cross[jj // 2, gg].astype(F32)
+
+            @pl.when(has_above)
+            def _():
+                kv_down(jj, gg).wait_recv()
+                d_kv[rows_of] = d_kv[rows_of] + chain[jj // 2, gg].astype(F32)
+
+        settled = n - whole_head
+
+        @pl.when((settled >= 0) & (settled % blocks == 0) & (settled // blocks < KVH))
+        def _():
+            finish_head(settled // blocks)
+
+        serve(n, 0, end)
+
+        @pl.when(n == end - 1)
+        def _():
+            tail_cube.step(*late(KVH - 1), 0)
+
         return carry
 
-    lax.fori_loop(0, slots, slot, 0)
+    lax.fori_loop(0, end, slot, 0)
 
     def drain_backward(n, carry):
         j, g = n // KVH, n % KVH
@@ -606,90 +726,113 @@
     x = tokens[...].astype(F32)
     r1 = inverse_rms(x)
     weight = column(gain1[...])
-    normed = (x * r1 * weight).astype(BF16)
-    c, sn = cos[...], -sin[...]
-    nq, nk = H * HD, KVH * HD
-    turned = d_out
-    for h in range(H):
-        piece = dq[h // GROUP, h % GROUP] * HD**-0.5
-        turned[h * HD : (h + 1) * HD, :] = turn(piece, c, sn).astype(BF16)
+    d_normed = jnp.zeros_like(x)
     for g in range(KVH):
-        turned[nq + g * HD : nq + (g + 1) * HD, :] = turn(d_kv[g * PAIR : g * PAIR + HD], c, sn).astype(BF16)
-        turned[nq + nk + g * HD : nq + nk + (g + 1) * HD, :] = d_kv[g * PAIR + HD : (g + 1) * PAIR].astype(BF16)
-    d_normed = (
-        nn(wq[...], turned[:nq, :])
-        + nn(wk[...].T, turned[nq : nq + nk, :])
-        + nn(wv[...].T, turned[nq + nk : nq + 2 * nk, :])
-    )
-    query_grad = nt(normed, turned[:nq, :])
-    kv_grad = nt(turned[nq : nq + 2 * nk, :], normed)
-    gain1_grad = jnp.sum(d_normed * x * r1, axis=1, keepdims=True)
-    for i in range(4):
-        tail[0, i * width : (i + 1) * width] = query_grad[:, i * LANES : (i + 1) * LANES].astype(BF16)
-    tail[0, 4 * width :] = jnp.zeros((tail.shape[1] - 4 * width, LANES), BF16)
-    tail[1, :width] = with_gain(query_grad, gain1_grad)
-    for i in range(5):
-        first = width + i * 2 * nk
-        left = kv_grad[:, i * LANES : (i + 1) * LANES].astype(BF16)
-        if left.shape[1] < LANES:
-            left = jnp.concatenate([left, jnp.zeros_like(left)], axis=1)
-        tail[1, first : first + 2 * nk] = left
-    filled = width + 10 * nk
-    tail[1, filled:] = jnp.zeros((tail.shape[1] - filled, LANES), BF16)
-    cube.scatter(tail, tail_landing, count, 0).start()
+        first = g * span
+        middle, last_row = first + GROUP * HD, first + (GROUP + 1) * HD
+        heads = slice(g * GROUP * HD, (g + 1) * GROUP * HD)
+        own_head = slice(g * HD, (g + 1) * HD)
+        d_normed = (
+            d_normed
+            + nn(wq[:, heads], d_out[first:middle])
+            + nn(wk[own_head].T, d_out[middle:last_row])
+            + nn(wv[own_head].T, d_out[last_row : last_row + HD])
+        )
+    pads = jnp.zeros((1, gains.shape[1] - width), F32)
+    for i, values in enumerate((jnp.sum(d_normed * x * r1, axis=1, keepdims=True), gain2_grad)):
+        gains[i : i + 1] = jnp.concatenate([as_row(values), pads], axis=1)
+    gains[2:] = jnp.zeros((gains.shape[0] - 2, gains.shape[1]), F32)
+
+    def gain_swap(d):
+        return pltpu.make_async_remote_copy(
+            src_ref=gains,
+            dst_ref=gain_landing.at[d],
+            send_sem=gain_send.at[d],
+            recv_sem=gain_recv.at[d],
+            device_id=cube.partners[d],
+            device_id_type=MESH,
+        )
+
+    gain_swap(0).start()
+    tail_cube.step(*late(KVH - 1), 1)
     gained = weight * d_normed
     input_grad[...] = (
         d_hidden[...] + r1 * gained - x * (r1 * r1 * r1) * jnp.mean(gained * x, axis=0, keepdims=True)
     )
-    for k in range(2 * depth):
-        cube.step(tail, tail_landing, count, k)
+    for k in range(2, cube.steps):
+        serve_now(end + k - 2)
+        if k - 2 < depth:
+            gain_swap(k - 2).wait()
+            gains[...] = gains[...] + gain_landing[k - 2]
+            if k - 1 < depth:
+                gain_swap(k - 1).start()
+        tail_cube.step(*late(KVH - 1), k)
     for i in range(count):
-        cube.drain(parts.at[i], i)
-    cube.drain(tail, count)
+        cube.drain(*main(i))
+    for i in range(KVH):
+        tail_cube.drain(*late(i))
 
 
 def unpack_kernel(
-    chunks, parts, tail, gate, up, down, output, query, key, value, gain1, gain2
+    chunks, parts, tails, gains, late_out, late_grad,
+    gate, up, down, output_hbm, query_hbm, key_hbm, value_hbm, gain1, gain2, layer_out, input_grad,
+    output, query, key, value, sems,
 ):
     i = pl.program_id(0)
     width = gate.shape[0]
-
-    @pl.when(i < chunks)
+    layer_out[...] = late_out[...]
+    input_grad[...] = late_grad[...]
+    small = ((output, output_hbm), (query, query_hbm), (key, key_hbm), (value, value_hbm))
+    copies = [pltpu.make_async_copy(a, b, sems.at[n]) for n, (a, b) in enumerate(small)]
+
+    @pl.when(i > 0)
     def _():
         for k, out in enumerate((gate, up, down)):
             for half in range(2):
                 piece = parts[0, half, k * width : (k + 1) * width]
                 out[:, half * LANES : (half + 1) * LANES] = piece.astype(F32)
 
-    @pl.when(i == chunks)
+    def five(ref, at, rows):
+        half = rows // 2
+        yield ref[at + (0, slice(0, rows))]
+        yield ref[at + (0, slice(rows, 2 * rows))]
+        yield jnp.concatenate(
+            [ref[at + (0, slice(2 * rows, 2 * rows + half))], ref[at + (1, slice(0, half))]], axis=0
+        )
+        yield ref[at + (1, slice(half, half + rows))]
+        yield ref[at + (1, slice(half + rows, half + 2 * rows))]
+
+    @pl.when(i == 0)
     def _():
-        half = width // 2
-        output[:, :LANES] = parts[0, 0, :width].astype(F32)
-        output[:, LANES : 2 * LANES] = parts[0, 0, width : 2 * width].astype(F32)
-        output[:half, 2 * LANES : 3 * LANES] = parts[0, 0, 2 * width : 2 * width + half].astype(F32)
-        output[half:, 2 * LANES : 3 * LANES] = parts[0, 1, :half].astype(F32)
-        output[:, 3 * LANES : 4 * LANES] = parts[0, 1, half : half + width].astype(F32)
-        end = parts[0, 1, half + width : half + 2 * width].astype(F32)
-        output[:, 4 * LANES :] = end[:, :HD]
-        gain2[...] = end.T[HD : HD + 1]
-        for k in range(4):
-            query[:, k * LANES : (k + 1) * LANES] = tail[0, k * width : (k + 1) * width].astype(F32)
-        end = tail[1, :width].astype(F32)
-        query[:, 4 * LANES :] = end[:, :HD]
-        gain1[...] = end.T[HD : HD + 1]
-        nk = key.shape[0]
+        for k, block in enumerate(five(parts, (0,), width)):
+            size = min(LANES, width - k * LANES)
+            output[:, k * LANES : k * LANES + size] = block.astype(F32)[:, :size]
+        high = GROUP * HD
         for k in range(5):
             size = min(LANES, width - k * LANES)
             lanes = slice(k * LANES, k * LANES + size)
-            first = width + 2 * k * nk
-            key[:, lanes] = tail[1, first : first + nk].astype(F32)[:, :size]
-            value[:, lanes] = tail[1, first + nk : first + 2 * nk].astype(F32)[:, :size]
-
-
-def with_gain(grad, gain):
-    rows = grad.shape[0]
+            columns = []
+            for g in range(KVH):
+                block = list(five(tails, (g,), high + PAIR))[k].astype(F32)[:, :size]
+                own = slice(g * HD, (g + 1) * HD)
+                key[own, lanes] = block[high : high + HD]
+                value[own, lanes] = block[high + HD :]
+                columns.append(block[:high])
+            query[lanes, :] = jnp.concatenate(columns, axis=0).T
+        gain1[...] = gains[0, :width]
+        gain2[...] = gains[1, :width]
+        for copy in copies:
+            copy.start()
+
+    @pl.when(i == chunks)
+    def _():
+        for copy in copies:
+            copy.wait()
+
+
+def last_block(grad):
     return jnp.concatenate(
-        [grad[:, 4 * LANES :], gain, jnp.zeros((rows, LANES - HD - 1), F32)], axis=1
+        [grad[:, 4 * LANES :], jnp.zeros((grad.shape[0], LANES - HD), F32)], axis=1
     ).astype(BF16)
 
 
@@ -707,8 +850,9 @@
 
     chunks = ff // (2 * LANES)
     count = chunks + 1
-    part_rows = padded_rows(3 * width, depth)
-    tail_rows = padded_rows(max(4 * width, width + 10 * nk), depth)
+    part_rows = padded_rows(3 * width)
+    tail_rows = padded_rows(5 * (GROUP + 2) * HD // 2)
+    gain_shape = (8, 5 * LANES)
     vmem, smem, hbm = (pl.BlockSpec(memory_space=m) for m in (pltpu.VMEM, pltpu.SMEM, pl.ANY))
     head_t = (KVH, GROUP, PAIR, rows)
     head_o = (KVH, GROUP, HD, rows)
@@ -732,49 +876,63 @@
         dma((2, 3)),
         dma((2, blocks, KVH)),
         dma((blocks, KVH)),
-        dma((count + 1, 2 * depth)),
-        dma((count + 1, 2 * depth)),
-        pltpu.SemaphoreType.REGULAR((count + 1, depth)),
+        dma((count, depth + HALVINGS)),
+        dma((count, depth + HALVINGS)),
+        pltpu.SemaphoreType.REGULAR((count, HALVINGS)),
+        dma((KVH, depth + HALVINGS)),
+        dma((KVH, depth + HALVINGS)),
+        pltpu.SemaphoreType.REGULAR((KVH, HALVINGS)),
+        dma((depth,)),
+        dma((depth,)),
         dma((blocks, KVH)),
         dma((blocks // 2, KVH)),
         dma((blocks // 2, KVH)),
     ]
-    scratch += [pltpu.VMEM((count, part_rows >> d, LANES), BF16) for d in range(depth)]
-    scratch += [pltpu.VMEM((tail_rows >> d, LANES), BF16) for d in range(depth)]
-    layer_out, input_grad, parts, tail = pl.pallas_call(
+    scratch += [pltpu.VMEM((depth,) + gain_shape, F32)]
+    scratch += [pltpu.VMEM((count, n, LANES), BF16) for n in row_counts(part_rows, depth)]
+    scratch += [pltpu.VMEM((KVH, n, LANES), BF16) for n in row_counts(tail_rows, depth)]
+    layer_out, input_grad, parts, tails, gains = pl.pallas_call(
         functools.partial(mega_kernel, sizes),
         out_shape=[
             jax.ShapeDtypeStruct((width, rows), BF16),
             jax.ShapeDtypeStruct((width, rows), F32),
             jax.ShapeDtypeStruct((count, 2, part_rows, LANES), BF16),
-            jax.ShapeDtypeStruct((2, tail_rows, LANES), BF16),
+            jax.ShapeDtypeStruct((KVH, 2, tail_rows, LANES), BF16),
+            jax.ShapeDtypeStruct(gain_shape, F32),
         ],
         in_specs=[smem] * 3 + [vmem] * 9 + [hbm] * 5,
-        out_specs=[vmem] * 4,
+        out_specs=[vmem] * 5,
         scratch_shapes=scratch,
         compiler_params=pltpu.CompilerParams(
             vmem_limit_bytes=VMEM_LIMIT, collective_id=0, has_side_effects=True
         ),
     )(
         keep_mask, keep_rate, exit_scales,
-        tokens, groups, gain1[None, :], gain2[None, :], wk, wv, wq, cos, sin,
+        tokens, groups, gain1, gain2, wk, wv, wq, cos, sin,
         wo, wg, wu, wd, cotangent,
     )
 
-    wide = pl.BlockSpec((width, 2 * LANES), lambda i: (0, jnp.minimum(i, chunks - 1)))
-    small = [(nq, width), (width, nq), (nk, width), (nk, width), (1, width), (1, width)]
-    gate_grad, up_grad, down_grad, output_grad, query_grad, key_grad, value_grad, gain1_grad, gain2_grad = pl.pallas_call(
+    wide = pl.BlockSpec((width, 2 * LANES), lambda i: (0, jnp.maximum(i - 1, 0)))
+    lines = pl.BlockSpec((width // chunks, rows), lambda i: (jnp.maximum(i - 1, 0), 0))
+    line = pl.BlockSpec((width,), lambda i: (0,))
+    small = [(nq, width), (width, nq), (nk, width), (nk, width)]
+    (gate_grad, up_grad, down_grad, output_grad, query_grad, key_grad, value_grad, gain1_grad, gain2_grad, layer_out, input_grad) = pl.pallas_call(
         functools.partial(unpack_kernel, chunks),
         grid=(count,),
         out_shape=[jax.ShapeDtypeStruct((width, ff), F32)] * 3
-        + [jax.ShapeDtypeStruct(shape, F32) for shape in small],
+        + [jax.ShapeDtypeStruct(shape, F32) for shape in small + [(width,), (width,)]]
+        + [jax.ShapeDtypeStruct((width, rows), t) for t in (BF16, F32)],
         in_specs=[
-            pl.BlockSpec((1, 2, part_rows, LANES), lambda i: (i, 0, 0, 0)),
-            pl.BlockSpec(tail.shape, lambda i: (0, 0, 0)),
+            pl.BlockSpec((1, 2, part_rows, LANES), lambda i: ((i + chunks) % count, 0, 0, 0)),
+            pl.BlockSpec(tails.shape, lambda i: (0,) * 4),
+            pl.BlockSpec(gain_shape, lambda i: (0, 0)),
+            lines,
+            lines,
         ],
-        out_specs=[wide] * 3 + [pl.BlockSpec(shape, lambda i: (0, 0)) for shape in small],
+        out_specs=[wide] * 3 + [hbm] * 4 + [line] * 2 + [lines] * 2,
+        scratch_shapes=[pltpu.VMEM(shape, F32) for shape in small] + [dma((4,))],
         compiler_params=pltpu.CompilerParams(vmem_limit_bytes=VMEM_LIMIT),
-    )(parts, tail)
+    )(parts, tails, gains, layer_out, input_grad)
     return (
         layer_out.T[None],
         input_grad.T[None],
@@ -785,8 +943,8 @@
         gate_grad,
         up_grad,
         down_grad.T,
-        gain1_grad[0],
-        gain2_grad[0],
+        gain1_grad,
+        gain2_grad,
     )
 
 

time: 214 us -> 198 us (0.925)
  Pallas kernels: 201 us -> 194 us
  local copies, waits for them, and re-layouts: 4.37 us -> 0 us
  other arithmetic: 4.33 us -> 1.66 us
    pallas_call x1, Pallas kernels: 190 us -> 182 us  [body(): pl.pallas_call(functools.partial(mega_kernel, sizes), out_shape=[jax.Shap...]
    pallas_call x2 -> x0, other arithmetic: 2.67 us -> none  [body(): pl.pallas_call(functools.partial(unpack_kernel, chunks), grid=(count,), o...]
    broadcast_in_dim x2 -> x0, local copies, waits for them, and re-layouts: 2.53 us -> none  [the longest x1 1.27 us: body(): gain1[None, :]]
where the time goes in v4:
time: 198 us; the launch traced here: 197 us
  Pallas kernels  194 us (98%)
  between operations  2.13 us (1%)
    pallas_call x1, Pallas kernels, body(): pl.pallas_call(functools.partial(mega_kernel, sizes), out_shape=[jax.Shap...  182 us
    pallas_call x1, Pallas kernels, body(): pl.pallas_call(functools.partial(unpack_kernel, chunks), grid=(count,), o...  11.1 us

profile of v4, /device:TPU:0, one launch (start us, length us, event | category | flops | bytes accessed | tf_op | source)
XLA Modules:
  0.0 197.4 jit_solution(3307626578887653729)
XLA Ops:
  1.9 0.7 convert_element_type.4
  2.6 1.0 multiply_sine_fusion
  3.6 182.5 %shard_map.239 = (bf16[576,512]{1,0:T(8,128)(2,1)}, f32[576,512]{1,0:T(8,128)}, bf16[7,2,1728,128]{3,2,1,0:T(8,128)(2,1)}, bf16[3,2,832,128]{3,2,1,0:T(8,128)(2,1)}, f32[8,640]{1,0:T(8,128)}) custom-call(s32[1]{0:T(128)S(6)} %copy.27.keep_mask, f32[1]{0:T(128)S(6)} %copy.28.keep_rate, f32[2]{0:T(128)} %exit_scales.1, bf16[576,512]{1,0:T(8,128)(2,1)} %bitcast.20, ...), custom_call_target="tpu_custom_call" | custom-call | tf_op jit(solution)/shard_map/pallas_call | solution.py:894
  186.1 11.1 %shard_map.240 = (f32[576,1536]{1,0:T(8,128)}, f32[576,1536]{1,0:T(8,128)}, f32[576,1536]{1,0:T(8,128)}, f32[576,576]{1,0:T(8,128)}, f32[576,576]{1,0:T(8,128)},...) custom-call(bf16[7,2,1728,128]{3,2,1,0:T(8,128)(2,1)} %get-tuple-ele, ...), custom_call_target="tpu_custom_call" | custom-call | tf_op jit(solution)/shard_map/pallas_call | solution.py:919
  (1 shorter events, 0.0 us)

commit v5 on v4

--- a/solution.py
+++ b/solution.py
@@ -24,6 +24,7 @@
 VMEM_LIMIT = 61 * 1024 * 1024
 MESH = pl.DeviceIdType.MESH
 LANES = 128
+REROUTED = 2
 
 
 def nn(a, b):
@@ -249,16 +250,17 @@
 
 
 MAIN_SLOTS = [
-    [-7, -5, -3, -1, 1, 4, 6, 8],
-    [-6, -4, -2, 0, 2, 5, 10, 12],
-    [-5, -2, 0, 2, 5, 7, 9, 11],
-    [-4, -1, 1, 3, 9, 11, 16, 20],
-    [-3, 0, 2, 4, 8, 10, 13, 23],
-    [1, 3, 7, 9, 13, 14, 17, 23],
-    [-1, 6, 8, 11, 14, 16, 20, 22],
+    [-7, -5, -4, -2, 0, 4, 15, 25],
+    [-6, -4, -2, 0, 2, 4, 6, 11],
+    [-5, -2, 0, 2, 6, 9, 21, 25],
+    [-4, -1, 2, 6, 10, 16, 30, 31],
+    [-3, 1, 2, 4, 7, 10, 13, 16],
+    [-1, 2, 5, 7, 12, 17, 23, 27],
+    [1, 4, 7, 12, 16, 22, 27, 30],
 ]
-LATE_SLOTS = [[13, 14, 16, 17, 18, 19, 22, 23], [18, 19, 20, 21, 22, 23, 25, 28]]
-LAGS = [7, 6, 3, 2]
+LATE_SLOTS = [[11, 14, 17, 19, 23, 24, 27, 30], [19, 21, 26, 27, 29, 30, 31, 32]]
+LAGS = [8, 6, 4, 2]
+Z_FIRST = [3]
 
 
 def tables(count, depth, blocks):
@@ -278,7 +280,7 @@
 
 def rounds(slots, first, last):
     lists = []
-    for i, n in enumerate(slots):
+    for i, n in slots:
         if first <= n < last:
             for chosen in lists:
                 if all(n != other for _, other in chosen):
@@ -321,12 +323,13 @@
     keep_mask, keep_rate, exit_scales,
     tokens, groups, gain1, gain2, wk, wv, wq, cos, sin,
     wo_hbm, wg_hbm, wu_hbm, wd_hbm, cot_hbm,
-    layer_out, input_grad, parts, tails, gains,
+    layer_out_hbm, input_grad_hbm, parts_hbm, tails, gains,
+    layer_out, input_grad, parts,
     wo, stream, cotangent,
     queries, kv_all, attended, mixed_t, top, total,
     d_normed2, d_out,
     chain, cross,
-    load_sem, stream_sem, send_sem, recv_sem, cube_send, cube_recv, credit, tail_send, tail_recv, tail_credit,
+    load_sem, stream_sem, out_sem, send_sem, recv_sem, cube_send, cube_recv, credit, tail_send, tail_recv, tail_credit,
     gain_send, gain_recv, kv_send, chain_recv, cross_recv, gain_landing,
     *landings,
 ):
@@ -337,6 +340,8 @@
     has_above, has_below = z < floors - 1, z > 0
     links = cube_links(s, b, sizes)
     cube = Cube(links, cube_send, cube_recv, credit)
+    z_links = links[:1] + links[3:] + links[1:3]
+    z_cube = Cube(z_links, cube_send, cube_recv, credit)
     tail_cube = Cube(links, tail_send, tail_recv, tail_credit)
     depth = cube.depth
     count = parts.shape[0]
@@ -397,6 +402,9 @@
             device_id_type=MESH,
         )
 
+    def rerouted(j, g):
+        return (j == 0) & (g < REROUTED)
+
     normed = normalize(tokens, gain1)
     c, sn = cos[...], sin[...]
     project_kv(normed, wk, wv, c, sn, kv_all.at[b])
@@ -433,13 +441,21 @@
                 def _():
                     copy(0, j, g).start()
 
-                copy(1, j, g).start()
+                @pl.when(jnp.logical_not(rerouted(j, g)))
+                def _():
+                    copy(1, j, g).start()
+
                 next_unit(g, queries, kv_all[j, g], attended, top, total)
 
             @pl.when((m >= 2) | (y == 1))
             def _():
                 j = b - 2 * m + 3 - 2 * y
                 copy(1, j, g).wait_recv()
+
+                @pl.when(has_above & rerouted(j, g))
+                def _():
+                    copy(0, j, g).start()
+
                 next_unit(g, queries, kv_all[j, g], attended, top, total)
 
             return inner
@@ -458,7 +474,7 @@
             def _():
                 copy(0, j, g).wait_send()
 
-            @pl.when((m >= 1) | (y == 0))
+            @pl.when(((m >= 1) & jnp.logical_not(rerouted(j, g))) | ((m == 0) & (y == 0)))
             def _():
                 copy(1, j, g).wait_send()
 
@@ -467,19 +483,32 @@
         return lax.fori_loop(0, KVH, one, carry)
 
     lax.fori_loop(0, z + 1, drain_forward, 0)
+
+    @pl.when(has_above & (y == 1))
+    def _():
+        for g in range(REROUTED):
+            copy(0, 0, g).wait_send()
+
 
     whole_head = 2 * floors + 1
     end = (KVH - 1) * blocks + whole_head + 2
     main_slots, late_slots, lags = tables(count, depth, blocks)
     lead = count + 1
+    rows_of_main = list(enumerate(main_slots))
+    plan = (
+        (tail_cube, late, list(enumerate(late_slots))),
+        (cube, main, [(i, row) for i, row in rows_of_main if i not in Z_FIRST]),
+        (z_cube, main, [(i, row) for i, row in rows_of_main if i in Z_FIRST]),
+    )
+
+    def part_out(i):
+        return pltpu.make_async_copy(parts.at[i], parts_hbm.at[i], out_sem.at[i])
+
 
     def serve(n, first, last):
         for k in range(cube.steps - 1, -1, -1):
-            for exchange, block_of, slots in (
-                (tail_cube, late, late_slots),
-                (cube, main, main_slots),
-            ):
-                for chosen in rounds([row[k] for row in slots], first, last):
+            for exchange, block_of, slots in plan:
+                for chosen in rounds([(i, row[k]) for i, row in slots], first, last):
                     found = at_slot(chosen, n)
 
                     @pl.when(found > 0)
@@ -488,13 +517,12 @@
 
     def serve_now(n):
         for k in range(cube.steps - 1, -1, -1):
-            for exchange, block_of, slots in (
-                (tail_cube, late, late_slots),
-                (cube, main, main_slots),
-            ):
-                for i, row in enumerate(slots):
+            for exchange, block_of, slots in plan:
+                for i, row in slots:
                     if row[k] == n or (n == end + cube.steps - 3 and row[k] > n):
                         exchange.step(*block_of(i), k)
+                        if block_of is main and n >= end and k == cube.steps - 1:
+                            part_out(i).start()
 
     for load in loads:
         load.wait()
@@ -552,6 +580,8 @@
 
     lax.fori_loop(0, chunks, chunk, 0)
     layer_out[...] = (hidden + bs * down[...]).astype(BF16)
+    whole_out = pltpu.make_async_copy(layer_out, layer_out_hbm, out_sem.at[count])
+    whole_out.start()
     dn = d_normed2[...]
     gain2_grad = jnp.sum(dn * hidden * r2, axis=1, keepdims=True)
     gained = gain * dn
@@ -754,11 +784,16 @@
         )
 
     gain_swap(0).start()
+    for i, row in rows_of_main:
+        if row[-1] < end:
+            part_out(i).start()
     tail_cube.step(*late(KVH - 1), 1)
     gained = weight * d_normed
     input_grad[...] = (
         d_hidden[...] + r1 * gained - x * (r1 * r1 * r1) * jnp.mean(gained * x, axis=0, keepdims=True)
     )
+    grad_out = pltpu.make_async_copy(input_grad, input_grad_hbm, out_sem.at[count + 1])
+    grad_out.start()
     for k in range(2, cube.steps):
         serve_now(end + k - 2)
         if k - 2 < depth:
@@ -768,7 +803,10 @@
                 gain_swap(k - 1).start()
         tail_cube.step(*late(KVH - 1), k)
     for i in range(count):
-        cube.drain(*main(i))
+        (z_cube if i in Z_FIRST else cube).drain(*main(i))
+        part_out(i).wait()
+    whole_out.wait()
+    grad_out.wait()
     for i in range(KVH):
         tail_cube.drain(*late(i))
 
@@ -859,6 +897,9 @@
     head_1 = (KVH, GROUP, 1, rows)
     dma = pltpu.SemaphoreType.DMA
     scratch = [
+        pltpu.VMEM((width, rows), BF16),
+        pltpu.VMEM((width, rows), F32),
+        pltpu.VMEM((count, 2, part_rows, LANES), BF16),
         pltpu.VMEM(wo.shape, BF16),
         pltpu.VMEM((2, 3, width, 2 * LANES), BF16),
         pltpu.VMEM(cotangent.shape, BF16),
@@ -874,6 +915,7 @@
         pltpu.VMEM((blocks // 2, KVH, PAIR, rows), BF16),
         dma((2,)),
         dma((2, 3)),
+        dma((count + 2,)),
         dma((2, blocks, KVH)),
         dma((blocks, KVH)),
         dma((count, depth + HALVINGS)),
@@ -901,7 +943,7 @@
             jax.ShapeDtypeStruct(gain_shape, F32),
         ],
         in_specs=[smem] * 3 + [vmem] * 9 + [hbm] * 5,
-        out_specs=[vmem] * 5,
+        out_specs=[hbm] * 3 + [vmem] * 2,
         scratch_shapes=scratch,
         compiler_params=pltpu.CompilerParams(
             vmem_limit_bytes=VMEM_LIMIT, collective_id=0, has_side_effects=True

time: 198 us -> 184 us (0.929)
  Pallas kernels: 194 us -> 180 us
    pallas_call x1, Pallas kernels: 182 us -> 169 us  [body(): pl.pallas_call(functools.partial(mega_kernel, sizes), out_shape=[jax.Shap...]
where the time goes in v5:
time: 184 us
  Pallas kernels  180 us (98%)
  between operations  2.13 us (1%)
    pallas_call x1, Pallas kernels, body(): pl.pallas_call(functools.partial(mega_kernel, sizes), out_shape=[jax.Shap...  169 us
    pallas_call x1, Pallas kernels, body(): pl.pallas_call(functools.partial(unpack_kernel, chunks), grid=(count,), o...  11.1 us

profile of v5, /device:TPU:0, one launch (start us, length us, event | category | flops | bytes accessed | tf_op | source)
XLA Modules:
  0.0 183.8 jit_solution(12795533218550821338)
XLA Ops:
  1.9 0.7 convert_element_type.4
  2.6 1.0 multiply_sine_fusion
  3.6 168.9 %shard_map.239 = (bf16[576,512]{1,0:T(8,128)(2,1)}, f32[576,512]{1,0:T(8,128)}, bf16[7,2,1728,128]{3,2,1,0:T(8,128)(2,1)}, bf16[3,2,832,128]{3,2,1,0:T(8,128)(2,1)}, f32[8,640]{1,0:T(8,128)}) custom-call(s32[1]{0:T(128)S(6)} %copy.27.keep_mask, f32[1]{0:T(128)S(6)} %copy.28.keep_rate, f32[2]{0:T(128)} %exit_scales.1, bf16[576,512]{1,0:T(8,128)(2,1)} %bitcast.20, ...), custom_call_target="tpu_custom_call" | custom-call | tf_op jit(solution)/shard_map/pallas_call | solution.py:936
  172.5 11.1 %shard_map.240 = (f32[576,1536]{1,0:T(8,128)}, f32[576,1536]{1,0:T(8,128)}, f32[576,1536]{1,0:T(8,128)}, f32[576,576]{1,0:T(8,128)}, f32[576,576]{1,0:T(8,128)},...) custom-call(bf16[7,2,1728,128]{3,2,1,0:T(8,128)(2,1)} %get-tuple-ele, ...), custom_call_target="tpu_custom_call" | custom-call | tf_op jit(solution)/shard_map/pallas_call | solution.py:961
  (1 shorter events, 0.0 us)

commit v6 on v5

--- a/solution.py
+++ b/solution.py
@@ -141,37 +141,52 @@
 
 def grad_unit(g, queries, d_out, lse, delta, packed, dq, masked):
     rows = queries.shape[-1]
+    part = rows // 2
     natural = packed.T
-
-    def d_head(r, first=0):
+    items = [(r, c) for r in range(GROUP) for c in range(2)]
+    columns = [slice(c * part, (c + 1) * part) for c in range(2)]
+    before = [dq[g, r, :, columns[c]] for r, c in items]
+
+    def seen(c):
+        return (c + 1) * part if masked else rows
+
+    def d_head(r, c, first=0):
         start = pl.multiple_of((g * GROUP + r) * PAIR + first, HD)
-        return d_out[pl.ds(start, PAIR - first)]
-
-    before = [dq[g, r] for r in range(GROUP)]
-
-    def products(r):
-        return nn(natural, queries[g, r]), nn(natural, d_head(r))
-
-    ahead = products(0)
+        return d_out[pl.ds(start, PAIR - first), columns[c]]
+
+    def products(r, c):
+        keys = natural[: seen(c)]
+        return nn(keys, queries[g, r, :, columns[c]]), nn(keys, d_head(r, c))
+
+    ahead = products(*items[0])
     done = []
-    d_keys, d_vals = None, None
-    for r in range(GROUP):
+    totals = [None] * 4
+    for i, (r, c) in enumerate(items):
         scores, d_probs = ahead
-        if r + 1 < GROUP:
-            ahead = products(r + 1)
-        probs = jnp.exp2(scores - lse[g, r])
+        if i + 1 < len(items):
+            ahead = products(*items[i + 1])
+        probs = jnp.exp2(scores - lse[g, r, :, columns[c]])
         if masked:
             key_at = lax.broadcasted_iota(jnp.int32, scores.shape, 0)
-            query_at = lax.broadcasted_iota(jnp.int32, scores.shape, 1)
+            query_at = lax.broadcasted_iota(jnp.int32, scores.shape, 1) + c * part
             probs = jnp.where(key_at <= query_at, probs, 0.0)
-        d_scores = (probs * (d_probs - delta[g, r])).astype(BF16)
-        keys_term = nt(queries[g, r, :HD], d_scores)
-        vals_term = nt(d_head(r, HD), probs.astype(BF16))
-        d_keys = keys_term if d_keys is None else d_keys + keys_term
-        d_vals = vals_term if d_vals is None else d_vals + vals_term
-        done.append(before[r] + nn(packed[:HD], d_scores))
-    for r in range(GROUP):
-        dq[g, r] = done[r]
+        d_scores = (probs * (d_probs - delta[g, r, :, columns[c]])).astype(BF16)
+        terms = (
+            nt(d_head(r, c, HD), probs.astype(BF16)),
+            nt(queries[g, r, :HD, columns[c]], d_scores),
+        )
+        kind = c if masked else 0
+        for n, term in enumerate(terms):
+            at = 2 * kind + n
+            totals[at] = term if totals[at] is None else totals[at] + term
+        done.append(before[i] + nn(packed[:HD, : seen(c)], d_scores))
+    for i, (r, c) in enumerate(items):
+        dq[g, r, :, columns[c]] = done[i]
+    d_vals, d_keys = totals[:2]
+    if masked:
+        rest = jnp.zeros((HD, rows - part), F32)
+        d_vals = totals[2] + jnp.concatenate([d_vals, rest], axis=1)
+        d_keys = totals[3] + jnp.concatenate([d_keys, rest], axis=1)
     return d_keys * LN2, d_vals
 
 
@@ -250,15 +265,15 @@
 
 
 MAIN_SLOTS = [
-    [-7, -5, -4, -2, 0, 4, 15, 25],
-    [-6, -4, -2, 0, 2, 4, 6, 11],
-    [-5, -2, 0, 2, 6, 9, 21, 25],
-    [-4, -1, 2, 6, 10, 16, 30, 31],
-    [-3, 1, 2, 4, 7, 10, 13, 16],
-    [-1, 2, 5, 7, 12, 17, 23, 27],
-    [1, 4, 7, 12, 16, 22, 27, 30],
+    [-7, -5, -4, -2, 0, 7, 22, 28],
+    [-6, -4, -2, 0, 2, 3, 7, 25],
+    [-5, -2, 0, 2, 7, 10, 31, 32],
+    [-4, -1, 2, 6, 10, 16, 25, 32],
+    [-3, 1, 2, 4, 9, 12, 23, 25],
+    [-1, 2, 4, 7, 14, 18, 25, 30],
+    [1, 3, 6, 11, 18, 22, 27, 29],
 ]
-LATE_SLOTS = [[11, 14, 17, 19, 23, 24, 27, 30], [19, 21, 26, 27, 29, 30, 31, 32]]
+LATE_SLOTS = [[12, 14, 17, 19, 23, 24, 27, 31], [21, 23, 26, 27, 29, 30, 31, 32]]
 LAGS = [8, 6, 4, 2]
 Z_FIRST = [3]
 
@@ -278,24 +293,13 @@
     return main, late, [2 * (floors - z) for z in range(floors)]
 
 
-def rounds(slots, first, last):
-    lists = []
-    for i, n in slots:
-        if first <= n < last:
-            for chosen in lists:
-                if all(n != other for _, other in chosen):
-                    chosen.append((i, n))
-                    break
-            else:
-                lists.append([(i, n)])
-    return lists
-
-
-def at_slot(chosen, n):
-    found = 0
-    for i, slot in chosen:
-        found = found + jnp.where(n == slot, i + 1, 0)
-    return found
+def by_slot(n, first, last, act):
+    if last - first == 1:
+        act(first)
+        return
+    middle = (first + last) // 2
+    for wanted, lo, hi in ((n < middle, first, middle), (n >= middle, middle, last)):
+        pl.when(wanted)(functools.partial(by_slot, n, lo, hi, act))
 
 
 def cube_links(s, b, sizes):
@@ -505,16 +509,6 @@
         return pltpu.make_async_copy(parts.at[i], parts_hbm.at[i], out_sem.at[i])
 
 
-    def serve(n, first, last):
-        for k in range(cube.steps - 1, -1, -1):
-            for exchange, block_of, slots in plan:
-                for chosen in rounds([(i, row[k]) for i, row in slots], first, last):
-                    found = at_slot(chosen, n)
-
-                    @pl.when(found > 0)
-                    def _(exchange=exchange, block_of=block_of, k=k, found=found):
-                        exchange.step(*block_of(jnp.maximum(found - 1, 0)), k)
-
     def serve_now(n):
         for k in range(cube.steps - 1, -1, -1):
             for exchange, block_of, slots in plan:
@@ -564,18 +558,20 @@
         sig = 1.0 / (1.0 + jnp.exp(-gate))
         silu = gate * sig
         act = (silu * up).astype(BF16)
+        down[...] += nt(wd[...], act)
+        down_grad = nn(d_down_t, act)
+        d_up = (d_act * silu).astype(BF16)
+        up_grad = nn(normed2_t, d_up)
         d_gate = (d_act * up * (sig + silu * (1.0 - sig))).astype(BF16)
-        d_up = (d_act * silu).astype(BF16)
-        grads = (nn(normed2_t, d_gate), nn(normed2_t, d_up), nn(d_down_t, act))
-        for k, value in enumerate(grads):
+        gate_grad = nn(normed2_t, d_gate)
+        d_normed2[...] += nt(wu[...], d_up) + nt(wg[...], d_gate)
+        for k, value in enumerate((gate_grad, up_grad, down_grad)):
             for half in range(2):
                 parts[f, half, k * width : (k + 1) * width] = value[
                     :, half * LANES : (half + 1) * LANES
                 ].astype(BF16)
-        down[...] += nt(wd[...], act)
-        d_normed2[...] += nt(wg[...], d_gate) + nt(wu[...], d_up)
         cube.begin(*main(f), 0)
-        serve(f - lead, -lead, -2)
+        by_slot(f, 0, chunks, lambda m: serve_now(m - lead))
         return carry
 
     lax.fori_loop(0, chunks, chunk, 0)
@@ -728,7 +724,7 @@
         def _():
             finish_head(settled // blocks)
 
-        serve(n, 0, end)
+        by_slot(n, 0, end, serve_now)
 
         @pl.when(n == end - 1)
         def _():

time: 184 us -> 179 us (0.973)
  Pallas kernels: 180 us -> 175 us
    pallas_call x1, Pallas kernels: 169 us -> 164 us  [body(): pl.pallas_call(functools.partial(mega_kernel, sizes), out_shape=[jax.Shap...]
where the time goes in v6:
time: 179 us
  Pallas kernels  175 us (98%)
  between operations  2.13 us (1%)
    pallas_call x1, Pallas kernels, body(): pl.pallas_call(functools.partial(mega_kernel, sizes), out_shape=[jax.Shap...  164 us
    pallas_call x1, Pallas kernels, body(): pl.pallas_call(functools.partial(unpack_kernel, chunks), grid=(count,), o...  11.1 us

profile of v6, /device:TPU:0, one launch (start us, length us, event | category | flops | bytes accessed | tf_op | source)
XLA Modules:
  0.0 179.0 jit_solution(13512789722484741953)
XLA Ops:
  1.9 0.7 convert_element_type.4
  2.6 1.0 multiply_sine_fusion
  3.6 164.1 %shard_map.239 = (bf16[576,512]{1,0:T(8,128)(2,1)}, f32[576,512]{1,0:T(8,128)}, bf16[7,2,1728,128]{3,2,1,0:T(8,128)(2,1)}, bf16[3,2,832,128]{3,2,1,0:T(8,128)(2,1)}, f32[8,640]{1,0:T(8,128)}) custom-call(s32[1]{0:T(128)S(6)} %copy.27.keep_mask, f32[1]{0:T(128)S(6)} %copy.28.keep_rate, f32[2]{0:T(128)} %exit_scales.1, bf16[576,512]{1,0:T(8,128)(2,1)} %bitcast.20, ...), custom_call_target="tpu_custom_call" | custom-call | tf_op jit(solution)/shard_map/pallas_call | solution.py:932
  167.7 11.1 %shard_map.240 = (f32[576,1536]{1,0:T(8,128)}, f32[576,1536]{1,0:T(8,128)}, f32[576,1536]{1,0:T(8,128)}, f32[576,576]{1,0:T(8,128)}, f32[576,576]{1,0:T(8,128)},...) custom-call(bf16[7,2,1728,128]{3,2,1,0:T(8,128)(2,1)} %get-tuple-ele, ...), custom_call_target="tpu_custom_call" | custom-call | tf_op jit(solution)/shard_map/pallas_call | solution.py:957
  (1 shorter events, 0.0 us)

commit v7 on v6

--- a/solution.py
+++ b/solution.py
@@ -24,7 +24,7 @@
 VMEM_LIMIT = 61 * 1024 * 1024
 MESH = pl.DeviceIdType.MESH
 LANES = 128
-REROUTED = 2
+REROUTED = 1
 
 
 def nn(a, b):

time: 179 us -> 177 us (0.989)
  Pallas kernels: 175 us -> 173 us
    pallas_call x1, Pallas kernels: 164 us -> 161 us  [body(): pl.pallas_call(functools.partial(mega_kernel, sizes), out_shape=[jax.Shap...]
where the time goes in v7:
time: 177 us; the launch traced here: 176 us
  Pallas kernels  173 us (98%)
  between operations  2.13 us (1%)
    pallas_call x1, Pallas kernels, body(): pl.pallas_call(functools.partial(mega_kernel, sizes), out_shape=[jax.Shap...  161 us
    pallas_call x1, Pallas kernels, body(): pl.pallas_call(functools.partial(unpack_kernel, chunks), grid=(count,), o...  11.1 us

profile of v7, /device:TPU:0, one launch (start us, length us, event | category | flops | bytes accessed | tf_op | source)
XLA Modules:
  0.0 176.3 jit_solution(14396807861017753614)
XLA Ops:
  1.9 0.7 convert_element_type.4
  2.6 1.0 multiply_sine_fusion
  3.6 161.4 %shard_map.239 = (bf16[576,512]{1,0:T(8,128)(2,1)}, f32[576,512]{1,0:T(8,128)}, bf16[7,2,1728,128]{3,2,1,0:T(8,128)(2,1)}, bf16[3,2,832,128]{3,2,1,0:T(8,128)(2,1)}, f32[8,640]{1,0:T(8,128)}) custom-call(s32[1]{0:T(128)S(6)} %copy.27.keep_mask, f32[1]{0:T(128)S(6)} %copy.28.keep_rate, f32[2]{0:T(128)} %exit_scales.1, bf16[576,512]{1,0:T(8,128)(2,1)} %bitcast.20, ...), custom_call_target="tpu_custom_call" | custom-call | tf_op jit(solution)/shard_map/pallas_call | solution.py:932
  165.0 11.1 %shard_map.240 = (f32[576,1536]{1,0:T(8,128)}, f32[576,1536]{1,0:T(8,128)}, f32[576,1536]{1,0:T(8,128)}, f32[576,576]{1,0:T(8,128)}, f32[576,576]{1,0:T(8,128)},...) custom-call(bf16[7,2,1728,128]{3,2,1,0:T(8,128)(2,1)} %get-tuple-ele, ...), custom_call_target="tpu_custom_call" | custom-call | tf_op jit(solution)/shard_map/pallas_call | solution.py:957
  (1 shorter events, 0.0 us)

commit v8 on v7

--- a/solution.py
+++ b/solution.py
@@ -407,7 +407,7 @@
         )
 
     def rerouted(j, g):
-        return (j == 0) & (g < REROUTED)
+        return (j == 0) & (g >= KVH - REROUTED)
 
     normed = normalize(tokens, gain1)
     c, sn = cos[...], sin[...]
@@ -490,7 +490,7 @@
 
     @pl.when(has_above & (y == 1))
     def _():
-        for g in range(REROUTED):
+        for g in range(KVH - REROUTED, KVH):
             copy(0, 0, g).wait_send()
 
 

time: 177 us -> 179 us (1.011)
  Pallas kernels: 173 us -> 175 us
    pallas_call x1, Pallas kernels: 161 us -> 164 us  [body(): pl.pallas_call(functools.partial(mega_kernel, sizes), out_shape=[jax.Shap...]
where the time goes in v8:
time: 179 us
  Pallas kernels  175 us (98%)
  between operations  2.13 us (1%)
    pallas_call x1, Pallas kernels, body(): pl.pallas_call(functools.partial(mega_kernel, sizes), out_shape=[jax.Shap...  164 us
    pallas_call x1, Pallas kernels, body(): pl.pallas_call(functools.partial(unpack_kernel, chunks), grid=(count,), o...  11.1 us

profile of v8, /device:TPU:0, one launch (start us, length us, event | category | flops | bytes accessed | tf_op | source)
XLA Modules:
  0.0 179.0 jit_solution(29154491564204428)
XLA Ops:
  1.9 0.7 convert_element_type.4
  2.6 1.0 multiply_sine_fusion
  3.6 164.1 %shard_map.239 = (bf16[576,512]{1,0:T(8,128)(2,1)}, f32[576,512]{1,0:T(8,128)}, bf16[7,2,1728,128]{3,2,1,0:T(8,128)(2,1)}, bf16[3,2,832,128]{3,2,1,0:T(8,128)(2,1)}, f32[8,640]{1,0:T(8,128)}) custom-call(s32[1]{0:T(128)S(6)} %copy.27.keep_mask, f32[1]{0:T(128)S(6)} %copy.28.keep_rate, f32[2]{0:T(128)} %exit_scales.1, bf16[576,512]{1,0:T(8,128)(2,1)} %bitcast.20, ...), custom_call_target="tpu_custom_call" | custom-call | tf_op jit(solution)/shard_map/pallas_call | solution.py:932
  167.7 11.1 %shard_map.240 = (f32[576,1536]{1,0:T(8,128)}, f32[576,1536]{1,0:T(8,128)}, f32[576,1536]{1,0:T(8,128)}, f32[576,576]{1,0:T(8,128)}, f32[576,576]{1,0:T(8,128)},...) custom-call(bf16[7,2,1728,128]{3,2,1,0:T(8,128)(2,1)} %get-tuple-ele, ...), custom_call_target="tpu_custom_call" | custom-call | tf_op jit(solution)/shard_map/pallas_call | solution.py:957
  (1 shorter events, 0.0 us)
